TPU v7x, 256 devices: a whole 4x4x8 slice. The times are simulated.
256 devices in a mesh: ctx: 32 (over z, x), ch: 8 (over y, core).
Axes of the slice: x: 4, y: 4, z: 8, core: 2. Of those that a mesh axis runs over, the one named last changes fastest.
Arguments:
- gate_signal: bfloat16 [8192, 4096], P('ctx', 'ch'), may hold values from -6 to 6
- key_signal: bfloat16 [8192, 4096], P('ctx', 'ch'), may hold values from -6 to 6
- value_signal: bfloat16 [8192, 4096], P('ctx', 'ch'), may hold values from -6 to 6
- pole_decay: float32 [16, 4096], P(None, 'ch'), may hold values from 0 to 1, as said below
- pole_angle: float32 [16, 4096], P(None, 'ch'), may hold values from -3.140625 to 3.140625
- residue_real: float32 [16, 4096], P(None, 'ch'), may hold values from -1 to 1
- residue_imag: float32 [16, 4096], P(None, 'ch'), may hold values from -1 to 1
- skip_gain: float32 [4096], P('ch'), may hold values from -4 to 4
- out_weight: bfloat16 [4096, 4096], P(None, 'ch'), may hold values from -0.09375 to 0.09375
Outputs:
- mixer_out: bfloat16 [8192, 4096], P('ctx', 'ch')
Inputs may be any that keep to these rules, and one draw needn't show every extreme that they name: `pole_decay`: every entry is positive.
All inputs are finite; a program needn't handle non-finite values.
Results may differ from a plain program's by a relative error of at most 0.019.
Values may be sent and summed in bfloat16 or wider, within the bound.
A program may use at most 128 MiB of HBM per device.

v0:
```python
import jax
import jax.numpy as jnp
from jax import lax
from jax.sharding import PartitionSpec as P

BLOCK = 64


PRECISE = lax.Precision.HIGHEST


def passed_along(value, axis, steps):
    count = lax.axis_size(axis)
    first, last = (max(0, -steps), min(count, count - steps))
    return lax.ppermute(value, axis, [(source, source + steps) for source in range(first, last)])


def powers(decays, angles, exponent):
    magnitude = jnp.exp(-exponent * decays)
    return jnp.stack(
        [magnitude * jnp.cos(exponent * angles), magnitude * jnp.sin(exponent * angles)]
    )


def complex_mul(former, latter):
    return jnp.stack(
        [
            former[0] * latter[0] - former[1] * latter[1],
            former[0] * latter[1] + former[1] * latter[0],
        ]
    )


def block_scan(block_sums, initial, block_step):

    def advance(current, addend):
        return (complex_mul(block_step, current) + addend, current)

    final_state, block_starts = lax.scan(advance, initial, jnp.moveaxis(block_sums, 1, 0))
    return (final_state, jnp.moveaxis(block_starts, 0, 1))


def carried(span_total, span_step):

    def link(link_index, incoming):
        outgoing = complex_mul(span_step, incoming) + span_total
        return passed_along(outgoing, "ctx", 1)

    return lax.fori_loop(0, lax.axis_size("ctx") - 1, link, jnp.zeros_like(span_total))


def per_device(
    gate_signal,
    key_signal,
    value_signal,
    pole_decay,
    pole_angle,
    residue_real,
    residue_imag,
    skip_gain,
    out_weight,
):
    tok_rows, chan_width = key_signal.shape
    count_blocks = tok_rows // BLOCK
    driving = key_signal.astype(jnp.float32) * value_signal.astype(jnp.float32)
    blocked = driving.reshape(count_blocks, BLOCK, chan_width)
    offsets = jnp.arange(BLOCK).astype(jnp.float32)[:, None, None]
    powers_table = powers(pole_decay, pole_angle, offsets)
    response = jnp.sum(residue_real * powers_table[0] - residue_imag * powers_table[1], axis=1)
    lag_index = jnp.arange(BLOCK)[:, None] - jnp.arange(BLOCK)[None, :]
    toeplitz = jnp.where(
        (lag_index >= 0)[:, :, None], response[jnp.clip(lag_index, 0, BLOCK - 1)], 0.0
    )
    inner_part = jnp.einsum("tsc,bsc->btc", toeplitz, blocked, precision=PRECISE)
    block_sums = jnp.einsum("kjmc,bjc->kbmc", powers_table[:, ::-1], blocked, precision=PRECISE)
    ahead_pow = powers(pole_decay, pole_angle, offsets + 1.0)
    kernel = jnp.stack(
        [
            residue_real * ahead_pow[0] - residue_imag * ahead_pow[1],
            -(residue_real * ahead_pow[1] + residue_imag * ahead_pow[0]),
        ]
    )
    block_step = powers(pole_decay, pole_angle, float(BLOCK))
    span_step = powers(pole_decay, pole_angle, float(tok_rows))
    block_index = jnp.arange(count_blocks).astype(jnp.float32)[:, None, None]
    local_out = inner_part + skip_gain * blocked
    back_pow = powers(pole_decay, pole_angle, (count_blocks - 1 - block_index) * BLOCK)
    span_total = jnp.sum(complex_mul(back_pow, block_sums), axis=1)
    incoming = carried(span_total, span_step)
    final_state, block_starts = block_scan(block_sums, incoming, block_step)
    long_out = local_out + jnp.einsum("kjmc,kbmc->bjc", kernel, block_starts, precision=PRECISE)
    gated_out = (gate_signal.astype(jnp.float32) * long_out.reshape(tok_rows, chan_width)).astype(
        jnp.bfloat16
    )
    summed = (
        lax.psum_scatter(
            lax.dot_general(
                out_weight, gated_out, (((1,), (1,)), ((), ())), preferred_element_type=jnp.float32
            ).astype(jnp.bfloat16),
            "ch",
            scatter_dimension=0,
            tiled=True,
        )
        .astype(jnp.float32)
        .T
    )
    return summed.astype(jnp.bfloat16)


def solution(mesh):
    return jax.shard_map(
        per_device,
        mesh=mesh,
        in_specs=(
            P("ctx", "ch"),
            P("ctx", "ch"),
            P("ctx", "ch"),
            P(None, "ch"),
            P(None, "ch"),
            P(None, "ch"),
            P(None, "ch"),
            P("ch"),
            P(None, "ch"),
        ),
        out_specs=P("ctx", "ch"),
        check_vma=False,
    )
```

profile of v0, /device:TPU:224, one launch (start us, length us, event | category | flops | bytes accessed | tf_op | source)
XLA Modules:
  0.0 562.7 jit_solution(18132200659889599633)
XLA Ops:
  11.2 9.4 %fusion.20 = f32[64,512]{1,0:T(8,128)S(1)} fusion(f32[16,512]{1,0:T(8,128)} %param.19, f32[16,512]{1,0:T(8,128)} %param.17, f32[64]{0:T(128)S(1)} %iota_convert_fusion, f32[16,512]{1,0:T(8,128)} %param.16, f32[64]{0:T(128)S(1)} %get-tuple-element.150, f32[16,512]{1,0:T(8,128)} %param.18), kind=kLoop, calls=%fused_computation.44 | loop fusion | flops 4161536 | bytes 262656 | tf_op jit(solution)/shard_map/reduce_sum | solution.py:69
  20.6 34.9 %multiply_subtract_fusion = (f32[1,64,16,512]{1,2,0,3:T(8,128)}, f32[1,64,16,512]{1,2,0,3:T(8,128)}, f32[1,64,16,512]{1,2,0,3:T(8,128)S(1)}, f32[1,64,16,512]{1,2,0,3:T(8,128)S(1)}) fusion(f32[16,512]{0,1:T(8,128)S(1)} %copy.91, f32[64]{0:T(128)S(1)} %get-tuple-element.149, f32[64]{0:T(128)S(1)} %fusion.30, f32[16,512]{0,1:T(8,128)S(1)} %copy.90, ...), kind=kLoop, calls=%fused_computation.36 | loop fusion | flops 7864320 | bytes 8520704 | tf_op jit(solution)/shard_map/sub | solution.py:79
  55.6 4.1 pad_maximum_fusion
  59.7 13.5 %rev.3 = f32[2,64,16,512]{1,2,0,3:T(8,128)} reverse(f32[2,64,16,512]{1,2,0,3:T(8,128)} %pad_maximum_fusion), dimensions={1} | reverse | bytes 8388608 | tf_op jit(solution)/shard_map/rev | solution.py:75
  74.7 62.8 %fusion.34 = f32[512,4,2,16]{3,1,2,0:T(4,128)S(1)} fusion(f32[4,64,512,1]{1,0,3,2:T(4,128)} %copy.94, f32[2,64,16,512]{1,2,0,3:T(8,128)} %rev.3), kind=kOutput, calls=%fused_computation.78 | convolution fusion | flops 50331648 | bytes 4980736 | tf_op jit(solution)/shard_map/kjmc,bjc->kbmc/dot_general | solution.py:75
  140.2 259.1 %while.22 = (s32[]{:T(128)}, f32[2,16,512]{2,1,0:T(8,128)S(1)}, f32[16,512]{1,0:T(8,128)S(1)}, f32[16,512]{1,0:T(8,128)S(1)}, f32[2,16,512]{2,1,0:T(8,128)S(1)}, /*index=5*/s32[]{:T(128)}) while((s32[]{:T(128)}, f32[2,16,512]{2,1,0:T(8,128)S(1)}, f32[16,512]{1,0:T(8,128)S(1)}, f32[16,512]{1,0:T(8,128)S(1)}, f32[2,16,512]{2,1,0:T(8,128)S(1)}, ...), condition=%wide.region_3.4_spmd, body=%wide.region_2.3_spmd.sunk | while | flops 81922 | bytes 655469 | solution.py:49
  140.2 3.4 collective-permute-start
  143.6 4.9 collective-permute-done
  150.5 6.3 %collective-permute-done = f32[2,16,512]{2,1,0:T(8,128)S(1)} collective-permute-done((f32[2,16,512]{2,1,0:T(8,128)S(1)}, f32[2,16,512]{2,1,0:T(8,128)S(1)}, u32[]{:S(2)}, u32[]{:S(2)}) %collective-permute-start) | collective-permute-done | bytes 65568 | tf_op jit(solution)/shard_map/while/body/eval_jaxpr/ppermute | solution.py:15
  158.8 6.3 %collective-permute-done = f32[2,16,512]{2,1,0:T(8,128)S(1)} collective-permute-done((f32[2,16,512]{2,1,0:T(8,128)S(1)}, f32[2,16,512]{2,1,0:T(8,128)S(1)}, u32[]{:S(2)}, u32[]{:S(2)}) %collective-permute-start) | collective-permute-done | bytes 65568 | tf_op jit(solution)/shard_map/while/body/eval_jaxpr/ppermute | solution.py:15
  167.1 6.3 %collective-permute-done = f32[2,16,512]{2,1,0:T(8,128)S(1)} collective-permute-done((f32[2,16,512]{2,1,0:T(8,128)S(1)}, f32[2,16,512]{2,1,0:T(8,128)S(1)}, u32[]{:S(2)}, u32[]{:S(2)}) %collective-permute-start) | collective-permute-done | bytes 65568 | tf_op jit(solution)/shard_map/while/body/eval_jaxpr/ppermute | solution.py:15
  175.4 6.3 %collective-permute-done = f32[2,16,512]{2,1,0:T(8,128)S(1)} collective-permute-done((f32[2,16,512]{2,1,0:T(8,128)S(1)}, f32[2,16,512]{2,1,0:T(8,128)S(1)}, u32[]{:S(2)}, u32[]{:S(2)}) %collective-permute-start) | collective-permute-done | bytes 65568 | tf_op jit(solution)/shard_map/while/body/eval_jaxpr/ppermute | solution.py:15
  183.7 6.8 %collective-permute-done = f32[2,16,512]{2,1,0:T(8,128)S(1)} collective-permute-done((f32[2,16,512]{2,1,0:T(8,128)S(1)}, f32[2,16,512]{2,1,0:T(8,128)S(1)}, u32[]{:S(2)}, u32[]{:S(2)}) %collective-permute-start) | collective-permute-done | bytes 65568 | tf_op jit(solution)/shard_map/while/body/eval_jaxpr/ppermute | solution.py:15
  192.4 6.3 %collective-permute-done = f32[2,16,512]{2,1,0:T(8,128)S(1)} collective-permute-done((f32[2,16,512]{2,1,0:T(8,128)S(1)}, f32[2,16,512]{2,1,0:T(8,128)S(1)}, u32[]{:S(2)}, u32[]{:S(2)}) %collective-permute-start) | collective-permute-done | bytes 65568 | tf_op jit(solution)/shard_map/while/body/eval_jaxpr/ppermute | solution.py:15
  198.8 1.9 collective-permute-start
  200.7 6.3 %collective-permute-done = f32[2,16,512]{2,1,0:T(8,128)S(1)} collective-permute-done((f32[2,16,512]{2,1,0:T(8,128)S(1)}, f32[2,16,512]{2,1,0:T(8,128)S(1)}, u32[]{:S(2)}, u32[]{:S(2)}) %collective-permute-start) | collective-permute-done | bytes 65568 | tf_op jit(solution)/shard_map/while/body/eval_jaxpr/ppermute | solution.py:15
  209.0 6.3 %collective-permute-done = f32[2,16,512]{2,1,0:T(8,128)S(1)} collective-permute-done((f32[2,16,512]{2,1,0:T(8,128)S(1)}, f32[2,16,512]{2,1,0:T(8,128)S(1)}, u32[]{:S(2)}, u32[]{:S(2)}) %collective-permute-start) | collective-permute-done | bytes 65568 | tf_op jit(solution)/shard_map/while/body/eval_jaxpr/ppermute | solution.py:15
  215.4 1.9 collective-permute-start
  217.3 6.3 %collective-permute-done = f32[2,16,512]{2,1,0:T(8,128)S(1)} collective-permute-done((f32[2,16,512]{2,1,0:T(8,128)S(1)}, f32[2,16,512]{2,1,0:T(8,128)S(1)}, u32[]{:S(2)}, u32[]{:S(2)}) %collective-permute-start) | collective-permute-done | bytes 65568 | tf_op jit(solution)/shard_map/while/body/eval_jaxpr/ppermute | solution.py:15
  225.6 6.3 %collective-permute-done = f32[2,16,512]{2,1,0:T(8,128)S(1)} collective-permute-done((f32[2,16,512]{2,1,0:T(8,128)S(1)}, f32[2,16,512]{2,1,0:T(8,128)S(1)}, u32[]{:S(2)}, u32[]{:S(2)}) %collective-permute-start) | collective-permute-done | bytes 65568 | tf_op jit(solution)/shard_map/while/body/eval_jaxpr/ppermute | solution.py:15
  233.9 6.6 %collective-permute-done = f32[2,16,512]{2,1,0:T(8,128)S(1)} collective-permute-done((f32[2,16,512]{2,1,0:T(8,128)S(1)}, f32[2,16,512]{2,1,0:T(8,128)S(1)}, u32[]{:S(2)}, u32[]{:S(2)}) %collective-permute-start) | collective-permute-done | bytes 65568 | tf_op jit(solution)/shard_map/while/body/eval_jaxpr/ppermute | solution.py:15
  242.5 6.4 %collective-permute-done = f32[2,16,512]{2,1,0:T(8,128)S(1)} collective-permute-done((f32[2,16,512]{2,1,0:T(8,128)S(1)}, f32[2,16,512]{2,1,0:T(8,128)S(1)}, u32[]{:S(2)}, u32[]{:S(2)}) %collective-permute-start) | collective-permute-done | bytes 65568 | tf_op jit(solution)/shard_map/while/body/eval_jaxpr/ppermute | solution.py:15
  250.8 6.3 %collective-permute-done = f32[2,16,512]{2,1,0:T(8,128)S(1)} collective-permute-done((f32[2,16,512]{2,1,0:T(8,128)S(1)}, f32[2,16,512]{2,1,0:T(8,128)S(1)}, u32[]{:S(2)}, u32[]{:S(2)}) %collective-permute-start) | collective-permute-done | bytes 65568 | tf_op jit(solution)/shard_map/while/body/eval_jaxpr/ppermute | solution.py:15
  259.1 6.3 %collective-permute-done = f32[2,16,512]{2,1,0:T(8,128)S(1)} collective-permute-done((f32[2,16,512]{2,1,0:T(8,128)S(1)}, f32[2,16,512]{2,1,0:T(8,128)S(1)}, u32[]{:S(2)}, u32[]{:S(2)}) %collective-permute-start) | collective-permute-done | bytes 65568 | tf_op jit(solution)/shard_map/while/body/eval_jaxpr/ppermute | solution.py:15
  267.4 6.3 %collective-permute-done = f32[2,16,512]{2,1,0:T(8,128)S(1)} collective-permute-done((f32[2,16,512]{2,1,0:T(8,128)S(1)}, f32[2,16,512]{2,1,0:T(8,128)S(1)}, u32[]{:S(2)}, u32[]{:S(2)}) %collective-permute-start) | collective-permute-done | bytes 65568 | tf_op jit(solution)/shard_map/while/body/eval_jaxpr/ppermute | solution.py:15
  275.7 6.3 %collective-permute-done = f32[2,16,512]{2,1,0:T(8,128)S(1)} collective-permute-done((f32[2,16,512]{2,1,0:T(8,128)S(1)}, f32[2,16,512]{2,1,0:T(8,128)S(1)}, u32[]{:S(2)}, u32[]{:S(2)}) %collective-permute-start) | collective-permute-done | bytes 65568 | tf_op jit(solution)/shard_map/while/body/eval_jaxpr/ppermute | solution.py:15
  284.0 6.3 %collective-permute-done = f32[2,16,512]{2,1,0:T(8,128)S(1)} collective-permute-done((f32[2,16,512]{2,1,0:T(8,128)S(1)}, f32[2,16,512]{2,1,0:T(8,128)S(1)}, u32[]{:S(2)}, u32[]{:S(2)}) %collective-permute-start) | collective-permute-done | bytes 65568 | tf_op jit(solution)/shard_map/while/body/eval_jaxpr/ppermute | solution.py:15
  292.3 7.0 %collective-permute-done = f32[2,16,512]{2,1,0:T(8,128)S(1)} collective-permute-done((f32[2,16,512]{2,1,0:T(8,128)S(1)}, f32[2,16,512]{2,1,0:T(8,128)S(1)}, u32[]{:S(2)}, u32[]{:S(2)}) %collective-permute-start) | collective-permute-done | bytes 65568 | tf_op jit(solution)/shard_map/while/body/eval_jaxpr/ppermute | solution.py:15
  301.3 6.3 %collective-permute-done = f32[2,16,512]{2,1,0:T(8,128)S(1)} collective-permute-done((f32[2,16,512]{2,1,0:T(8,128)S(1)}, f32[2,16,512]{2,1,0:T(8,128)S(1)}, u32[]{:S(2)}, u32[]{:S(2)}) %collective-permute-start) | collective-permute-done | bytes 65568 | tf_op jit(solution)/shard_map/while/body/eval_jaxpr/ppermute | solution.py:15
  309.6 6.3 %collective-permute-done = f32[2,16,512]{2,1,0:T(8,128)S(1)} collective-permute-done((f32[2,16,512]{2,1,0:T(8,128)S(1)}, f32[2,16,512]{2,1,0:T(8,128)S(1)}, u32[]{:S(2)}, u32[]{:S(2)}) %collective-permute-start) | collective-permute-done | bytes 65568 | tf_op jit(solution)/shard_map/while/body/eval_jaxpr/ppermute | solution.py:15
  317.9 6.3 %collective-permute-done = f32[2,16,512]{2,1,0:T(8,128)S(1)} collective-permute-done((f32[2,16,512]{2,1,0:T(8,128)S(1)}, f32[2,16,512]{2,1,0:T(8,128)S(1)}, u32[]{:S(2)}, u32[]{:S(2)}) %collective-permute-start) | collective-permute-done | bytes 65568 | tf_op jit(solution)/shard_map/while/body/eval_jaxpr/ppermute | solution.py:15
  326.2 6.3 %collective-permute-done = f32[2,16,512]{2,1,0:T(8,128)S(1)} collective-permute-done((f32[2,16,512]{2,1,0:T(8,128)S(1)}, f32[2,16,512]{2,1,0:T(8,128)S(1)}, u32[]{:S(2)}, u32[]{:S(2)}) %collective-permute-start) | collective-permute-done | bytes 65568 | tf_op jit(solution)/shard_map/while/body/eval_jaxpr/ppermute | solution.py:15
  334.5 6.3 %collective-permute-done = f32[2,16,512]{2,1,0:T(8,128)S(1)} collective-permute-done((f32[2,16,512]{2,1,0:T(8,128)S(1)}, f32[2,16,512]{2,1,0:T(8,128)S(1)}, u32[]{:S(2)}, u32[]{:S(2)}) %collective-permute-start) | collective-permute-done | bytes 65568 | tf_op jit(solution)/shard_map/while/body/eval_jaxpr/ppermute | solution.py:15
  342.8 6.6 %collective-permute-done = f32[2,16,512]{2,1,0:T(8,128)S(1)} collective-permute-done((f32[2,16,512]{2,1,0:T(8,128)S(1)}, f32[2,16,512]{2,1,0:T(8,128)S(1)}, u32[]{:S(2)}, u32[]{:S(2)}) %collective-permute-start) | collective-permute-done | bytes 65568 | tf_op jit(solution)/shard_map/while/body/eval_jaxpr/ppermute | solution.py:15
  351.4 6.3 %collective-permute-done = f32[2,16,512]{2,1,0:T(8,128)S(1)} collective-permute-done((f32[2,16,512]{2,1,0:T(8,128)S(1)}, f32[2,16,512]{2,1,0:T(8,128)S(1)}, u32[]{:S(2)}, u32[]{:S(2)}) %collective-permute-start) | collective-permute-done | bytes 65568 | tf_op jit(solution)/shard_map/while/body/eval_jaxpr/ppermute | solution.py:15
  359.7 6.3 %collective-permute-done = f32[2,16,512]{2,1,0:T(8,128)S(1)} collective-permute-done((f32[2,16,512]{2,1,0:T(8,128)S(1)}, f32[2,16,512]{2,1,0:T(8,128)S(1)}, u32[]{:S(2)}, u32[]{:S(2)}) %collective-permute-start) | collective-permute-done | bytes 65568 | tf_op jit(solution)/shard_map/while/body/eval_jaxpr/ppermute | solution.py:15
  368.0 6.3 %collective-permute-done = f32[2,16,512]{2,1,0:T(8,128)S(1)} collective-permute-done((f32[2,16,512]{2,1,0:T(8,128)S(1)}, f32[2,16,512]{2,1,0:T(8,128)S(1)}, u32[]{:S(2)}, u32[]{:S(2)}) %collective-permute-start) | collective-permute-done | bytes 65568 | tf_op jit(solution)/shard_map/while/body/eval_jaxpr/ppermute | solution.py:15
  376.3 6.3 %collective-permute-done = f32[2,16,512]{2,1,0:T(8,128)S(1)} collective-permute-done((f32[2,16,512]{2,1,0:T(8,128)S(1)}, f32[2,16,512]{2,1,0:T(8,128)S(1)}, u32[]{:S(2)}, u32[]{:S(2)}) %collective-permute-start) | collective-permute-done | bytes 65568 | tf_op jit(solution)/shard_map/while/body/eval_jaxpr/ppermute | solution.py:15
  384.6 6.3 %collective-permute-done = f32[2,16,512]{2,1,0:T(8,128)S(1)} collective-permute-done((f32[2,16,512]{2,1,0:T(8,128)S(1)}, f32[2,16,512]{2,1,0:T(8,128)S(1)}, u32[]{:S(2)}, u32[]{:S(2)}) %collective-permute-start) | collective-permute-done | bytes 65568 | tf_op jit(solution)/shard_map/while/body/eval_jaxpr/ppermute | solution.py:15
  392.9 6.3 %collective-permute-done = f32[2,16,512]{2,1,0:T(8,128)S(1)} collective-permute-done((f32[2,16,512]{2,1,0:T(8,128)S(1)}, f32[2,16,512]{2,1,0:T(8,128)S(1)}, u32[]{:S(2)}, u32[]{:S(2)}) %collective-permute-start) | collective-permute-done | bytes 65568 | tf_op jit(solution)/shard_map/while/body/eval_jaxpr/ppermute | solution.py:15
  399.2 2.7 while.23
  402.0 1.9 copy.92
  403.9 10.5 %fusion.23 = f32[512,4,64]{2,1,0:T(4,128)} fusion(f32[2,4,16,512]{2,1,0,3:T(4,128)S(1)} %copy.92, f32[1,64,16,512]{1,2,0,3:T(8,128)} %get-tuple-element.138, f32[1,64,16,512]{1,2,0,3:T(8,128)} %get-tuple-element.137), kind=kOutput, calls=%fused_computation.47 | convolution fusion | flops 51380224 | bytes 4980736 | tf_op jit(solution)/shard_map/kjmc,kbmc->bjc/dot_general | solution.py:91
  416.1 17.0 %gather_fusion = f32[4096,512]{1,0:T(8,128)} fusion(f32[64,512]{1,0:T(8,128)S(1)} %fusion.20, s32[4096]{0:T(1024)S(1)} %broadcast_clamp_fusion), kind=kCustom, calls=%fused_computation | custom fusion | bytes 16793600 | tf_op jit(solution)/shard_map/gather | solution.py:72
  433.0 16.3 %copy.80 = f32[64,64,512]{1,0,2:T(8,128)} copy(f32[64,64,512]{2,1,0:T(8,128)} %bitcast.75) | data formatting | bytes 16777216 | tf_op jit(solution)/shard_map/gather | solution.py:72
  449.7 29.0 %fusion.4 = f32[512,4,64]{2,1,0:T(4,128)S(1)} fusion(f32[4,64,512]{1,0,2:T(4,128)S(1)} %copy.81, f32[64,64,512]{1,0,2:T(8,128)} %copy.80, pred[64,64]{1,0:T(8,128)(4,1)S(1)} %subtract_compare_fusion), kind=kOutput, calls=%fused_computation.16 | convolution fusion | flops 102760448 | bytes 9441280 | tf_op jit(solution)/shard_map/tsc,bsc->btc/dot_general | solution.py:74
  479.4 4.9 fusion.12
  484.3 71.4 %reduce-scatter.2.cloned.1.call-done = bf16[512,256]{0,1:T(8,128)(2,1)} async-done(((bf16[4096,256]{0,1:T(8,128)(2,1)}), bf16[512,256]{0,1:T(8,128)(2,1)}) %reduce-scatter.2.cloned.1.call-update) | async-done | bytes 262160 | tf_op jit(solution)/shard_map/reduce_scatter | solution.py:96
  (142 shorter events, 68.5 us)
Async XLA Ops:
  6.5 549.1 %reduce-scatter.2.cloned.1.call-start = ((), (), s32[]{:S(2)}) async-start(), calls=%async_computation.1 | async-start | bytes 2359296 | tf_op jit(solution)/shard_map/reduce_scatter | solution.py:96
  59.7 13.5 %copy-start.2 = (bf16[256,512]{1,0:T(8,128)(2,1)S(1)}, bf16[256,512]{1,0:T(8,128)(2,1)}, u32[]{:S(2)}) copy-start(bf16[256,512]{1,0:T(8,128)(2,1)} %param.15) | copy-start | bytes 786436
  59.7 13.5 %copy-start.3 = (bf16[256,512]{1,0:T(8,128)(2,1)S(1)}, bf16[256,512]{1,0:T(8,128)(2,1)}, u32[]{:S(2)}) copy-start(bf16[256,512]{1,0:T(8,128)(2,1)} %param.14) | copy-start | bytes 786436
  137.5 2.0 copy-start
  137.5 2.0 copy-start.1
  140.2 8.3 %collective-permute-start = (f32[2,16,512]{2,1,0:T(8,128)S(1)}, f32[2,16,512]{2,1,0:T(8,128)S(1)}, u32[]{:S(2)}, u32[]{:S(2)}) collective-permute-start(f32[2,16,512]{2,1,0:T(8,128)S(1)} %maximum_add_fusion.4), channel_id=1, source_target_pairs={{0,8},{8,16},{16,24},{24,32},{32,40},{40,48},{48,56},{56,64},{64,7... | collective-permute-start | bytes 196616 | tf_op jit(solution)/shard_map/while/body/eval_jaxpr/ppermute | solution.py:15
  148.5 8.3 %collective-permute-start = (f32[2,16,512]{2,1,0:T(8,128)S(1)}, f32[2,16,512]{2,1,0:T(8,128)S(1)}, u32[]{:S(2)}, u32[]{:S(2)}) collective-permute-start(f32[2,16,512]{2,1,0:T(8,128)S(1)} %maximum_add_fusion.4), channel_id=1, source_target_pairs={{0,8},{8,16},{16,24},{24,32},{32,40},{40,48},{48,56},{56,64},{64,7... | collective-permute-start | bytes 196616 | tf_op jit(solution)/shard_map/while/body/eval_jaxpr/ppermute | solution.py:15
  156.8 8.3 %collective-permute-start = (f32[2,16,512]{2,1,0:T(8,128)S(1)}, f32[2,16,512]{2,1,0:T(8,128)S(1)}, u32[]{:S(2)}, u32[]{:S(2)}) collective-permute-start(f32[2,16,512]{2,1,0:T(8,128)S(1)} %maximum_add_fusion.4), channel_id=1, source_target_pairs={{0,8},{8,16},{16,24},{24,32},{32,40},{40,48},{48,56},{56,64},{64,7... | collective-permute-start | bytes 196616 | tf_op jit(solution)/shard_map/while/body/eval_jaxpr/ppermute | solution.py:15
  165.1 8.3 %collective-permute-start = (f32[2,16,512]{2,1,0:T(8,128)S(1)}, f32[2,16,512]{2,1,0:T(8,128)S(1)}, u32[]{:S(2)}, u32[]{:S(2)}) collective-permute-start(f32[2,16,512]{2,1,0:T(8,128)S(1)} %maximum_add_fusion.4), channel_id=1, source_target_pairs={{0,8},{8,16},{16,24},{24,32},{32,40},{40,48},{48,56},{56,64},{64,7... | collective-permute-start | bytes 196616 | tf_op jit(solution)/shard_map/while/body/eval_jaxpr/ppermute | solution.py:15
  173.4 8.3 %collective-permute-start = (f32[2,16,512]{2,1,0:T(8,128)S(1)}, f32[2,16,512]{2,1,0:T(8,128)S(1)}, u32[]{:S(2)}, u32[]{:S(2)}) collective-permute-start(f32[2,16,512]{2,1,0:T(8,128)S(1)} %maximum_add_fusion.4), channel_id=1, source_target_pairs={{0,8},{8,16},{16,24},{24,32},{32,40},{40,48},{48,56},{56,64},{64,7... | collective-permute-start | bytes 196616 | tf_op jit(solution)/shard_map/while/body/eval_jaxpr/ppermute | solution.py:15
  181.7 8.7 %collective-permute-start = (f32[2,16,512]{2,1,0:T(8,128)S(1)}, f32[2,16,512]{2,1,0:T(8,128)S(1)}, u32[]{:S(2)}, u32[]{:S(2)}) collective-permute-start(f32[2,16,512]{2,1,0:T(8,128)S(1)} %maximum_add_fusion.4), channel_id=1, source_target_pairs={{0,8},{8,16},{16,24},{24,32},{32,40},{40,48},{48,56},{56,64},{64,7... | collective-permute-start | bytes 196616 | tf_op jit(solution)/shard_map/while/body/eval_jaxpr/ppermute | solution.py:15
  190.5 8.3 %collective-permute-start = (f32[2,16,512]{2,1,0:T(8,128)S(1)}, f32[2,16,512]{2,1,0:T(8,128)S(1)}, u32[]{:S(2)}, u32[]{:S(2)}) collective-permute-start(f32[2,16,512]{2,1,0:T(8,128)S(1)} %maximum_add_fusion.4), channel_id=1, source_target_pairs={{0,8},{8,16},{16,24},{24,32},{32,40},{40,48},{48,56},{56,64},{64,7... | collective-permute-start | bytes 196616 | tf_op jit(solution)/shard_map/while/body/eval_jaxpr/ppermute | solution.py:15
  198.8 8.3 %collective-permute-start = (f32[2,16,512]{2,1,0:T(8,128)S(1)}, f32[2,16,512]{2,1,0:T(8,128)S(1)}, u32[]{:S(2)}, u32[]{:S(2)}) collective-permute-start(f32[2,16,512]{2,1,0:T(8,128)S(1)} %maximum_add_fusion.4), channel_id=1, source_target_pairs={{0,8},{8,16},{16,24},{24,32},{32,40},{40,48},{48,56},{56,64},{64,7... | collective-permute-start | bytes 196616 | tf_op jit(solution)/shard_map/while/body/eval_jaxpr/ppermute | solution.py:15
  207.1 8.3 %collective-permute-start = (f32[2,16,512]{2,1,0:T(8,128)S(1)}, f32[2,16,512]{2,1,0:T(8,128)S(1)}, u32[]{:S(2)}, u32[]{:S(2)}) collective-permute-start(f32[2,16,512]{2,1,0:T(8,128)S(1)} %maximum_add_fusion.4), channel_id=1, source_target_pairs={{0,8},{8,16},{16,24},{24,32},{32,40},{40,48},{48,56},{56,64},{64,7... | collective-permute-start | bytes 196616 | tf_op jit(solution)/shard_map/while/body/eval_jaxpr/ppermute | solution.py:15
  215.4 8.3 %collective-permute-start = (f32[2,16,512]{2,1,0:T(8,128)S(1)}, f32[2,16,512]{2,1,0:T(8,128)S(1)}, u32[]{:S(2)}, u32[]{:S(2)}) collective-permute-start(f32[2,16,512]{2,1,0:T(8,128)S(1)} %maximum_add_fusion.4), channel_id=1, source_target_pairs={{0,8},{8,16},{16,24},{24,32},{32,40},{40,48},{48,56},{56,64},{64,7... | collective-permute-start | bytes 196616 | tf_op jit(solution)/shard_map/while/body/eval_jaxpr/ppermute | solution.py:15
  223.7 8.3 %collective-permute-start = (f32[2,16,512]{2,1,0:T(8,128)S(1)}, f32[2,16,512]{2,1,0:T(8,128)S(1)}, u32[]{:S(2)}, u32[]{:S(2)}) collective-permute-start(f32[2,16,512]{2,1,0:T(8,128)S(1)} %maximum_add_fusion.4), channel_id=1, source_target_pairs={{0,8},{8,16},{16,24},{24,32},{32,40},{40,48},{48,56},{56,64},{64,7... | collective-permute-start | bytes 196616 | tf_op jit(solution)/shard_map/while/body/eval_jaxpr/ppermute | solution.py:15
  232.0 8.5 %collective-permute-start = (f32[2,16,512]{2,1,0:T(8,128)S(1)}, f32[2,16,512]{2,1,0:T(8,128)S(1)}, u32[]{:S(2)}, u32[]{:S(2)}) collective-permute-start(f32[2,16,512]{2,1,0:T(8,128)S(1)} %maximum_add_fusion.4), channel_id=1, source_target_pairs={{0,8},{8,16},{16,24},{24,32},{32,40},{40,48},{48,56},{56,64},{64,7... | collective-permute-start | bytes 196616 | tf_op jit(solution)/shard_map/while/body/eval_jaxpr/ppermute | solution.py:15
  240.5 8.3 %collective-permute-start = (f32[2,16,512]{2,1,0:T(8,128)S(1)}, f32[2,16,512]{2,1,0:T(8,128)S(1)}, u32[]{:S(2)}, u32[]{:S(2)}) collective-permute-start(f32[2,16,512]{2,1,0:T(8,128)S(1)} %maximum_add_fusion.4), channel_id=1, source_target_pairs={{0,8},{8,16},{16,24},{24,32},{32,40},{40,48},{48,56},{56,64},{64,7... | collective-permute-start | bytes 196616 | tf_op jit(solution)/shard_map/while/body/eval_jaxpr/ppermute | solution.py:15
  248.9 8.3 %collective-permute-start = (f32[2,16,512]{2,1,0:T(8,128)S(1)}, f32[2,16,512]{2,1,0:T(8,128)S(1)}, u32[]{:S(2)}, u32[]{:S(2)}) collective-permute-start(f32[2,16,512]{2,1,0:T(8,128)S(1)} %maximum_add_fusion.4), channel_id=1, source_target_pairs={{0,8},{8,16},{16,24},{24,32},{32,40},{40,48},{48,56},{56,64},{64,7... | collective-permute-start | bytes 196616 | tf_op jit(solution)/shard_map/while/body/eval_jaxpr/ppermute | solution.py:15
  257.2 8.3 %collective-permute-start = (f32[2,16,512]{2,1,0:T(8,128)S(1)}, f32[2,16,512]{2,1,0:T(8,128)S(1)}, u32[]{:S(2)}, u32[]{:S(2)}) collective-permute-start(f32[2,16,512]{2,1,0:T(8,128)S(1)} %maximum_add_fusion.4), channel_id=1, source_target_pairs={{0,8},{8,16},{16,24},{24,32},{32,40},{40,48},{48,56},{56,64},{64,7... | collective-permute-start | bytes 196616 | tf_op jit(solution)/shard_map/while/body/eval_jaxpr/ppermute | solution.py:15
  265.5 8.3 %collective-permute-start = (f32[2,16,512]{2,1,0:T(8,128)S(1)}, f32[2,16,512]{2,1,0:T(8,128)S(1)}, u32[]{:S(2)}, u32[]{:S(2)}) collective-permute-start(f32[2,16,512]{2,1,0:T(8,128)S(1)} %maximum_add_fusion.4), channel_id=1, source_target_pairs={{0,8},{8,16},{16,24},{24,32},{32,40},{40,48},{48,56},{56,64},{64,7... | collective-permute-start | bytes 196616 | tf_op jit(solution)/shard_map/while/body/eval_jaxpr/ppermute | solution.py:15
  273.8 8.3 %collective-permute-start = (f32[2,16,512]{2,1,0:T(8,128)S(1)}, f32[2,16,512]{2,1,0:T(8,128)S(1)}, u32[]{:S(2)}, u32[]{:S(2)}) collective-permute-start(f32[2,16,512]{2,1,0:T(8,128)S(1)} %maximum_add_fusion.4), channel_id=1, source_target_pairs={{0,8},{8,16},{16,24},{24,32},{32,40},{40,48},{48,56},{56,64},{64,7... | collective-permute-start | bytes 196616 | tf_op jit(solution)/shard_map/while/body/eval_jaxpr/ppermute | solution.py:15
  282.1 8.3 %collective-permute-start = (f32[2,16,512]{2,1,0:T(8,128)S(1)}, f32[2,16,512]{2,1,0:T(8,128)S(1)}, u32[]{:S(2)}, u32[]{:S(2)}) collective-permute-start(f32[2,16,512]{2,1,0:T(8,128)S(1)} %maximum_add_fusion.4), channel_id=1, source_target_pairs={{0,8},{8,16},{16,24},{24,32},{32,40},{40,48},{48,56},{56,64},{64,7... | collective-permute-start | bytes 196616 | tf_op jit(solution)/shard_map/while/body/eval_jaxpr/ppermute | solution.py:15
  290.4 8.9 %collective-permute-start = (f32[2,16,512]{2,1,0:T(8,128)S(1)}, f32[2,16,512]{2,1,0:T(8,128)S(1)}, u32[]{:S(2)}, u32[]{:S(2)}) collective-permute-start(f32[2,16,512]{2,1,0:T(8,128)S(1)} %maximum_add_fusion.4), channel_id=1, source_target_pairs={{0,8},{8,16},{16,24},{24,32},{32,40},{40,48},{48,56},{56,64},{64,7... | collective-permute-start | bytes 196616 | tf_op jit(solution)/shard_map/while/body/eval_jaxpr/ppermute | solution.py:15
  299.3 8.3 %collective-permute-start = (f32[2,16,512]{2,1,0:T(8,128)S(1)}, f32[2,16,512]{2,1,0:T(8,128)S(1)}, u32[]{:S(2)}, u32[]{:S(2)}) collective-permute-start(f32[2,16,512]{2,1,0:T(8,128)S(1)} %maximum_add_fusion.4), channel_id=1, source_target_pairs={{0,8},{8,16},{16,24},{24,32},{32,40},{40,48},{48,56},{56,64},{64,7... | collective-permute-start | bytes 196616 | tf_op jit(solution)/shard_map/while/body/eval_jaxpr/ppermute | solution.py:15
  307.6 8.3 %collective-permute-start = (f32[2,16,512]{2,1,0:T(8,128)S(1)}, f32[2,16,512]{2,1,0:T(8,128)S(1)}, u32[]{:S(2)}, u32[]{:S(2)}) collective-permute-start(f32[2,16,512]{2,1,0:T(8,128)S(1)} %maximum_add_fusion.4), channel_id=1, source_target_pairs={{0,8},{8,16},{16,24},{24,32},{32,40},{40,48},{48,56},{56,64},{64,7... | collective-permute-start | bytes 196616 | tf_op jit(solution)/shard_map/while/body/eval_jaxpr/ppermute | solution.py:15
  315.9 8.3 %collective-permute-start = (f32[2,16,512]{2,1,0:T(8,128)S(1)}, f32[2,16,512]{2,1,0:T(8,128)S(1)}, u32[]{:S(2)}, u32[]{:S(2)}) collective-permute-start(f32[2,16,512]{2,1,0:T(8,128)S(1)} %maximum_add_fusion.4), channel_id=1, source_target_pairs={{0,8},{8,16},{16,24},{24,32},{32,40},{40,48},{48,56},{56,64},{64,7... | collective-permute-start | bytes 196616 | tf_op jit(solution)/shard_map/while/body/eval_jaxpr/ppermute | solution.py:15
  324.2 8.3 %collective-permute-start = (f32[2,16,512]{2,1,0:T(8,128)S(1)}, f32[2,16,512]{2,1,0:T(8,128)S(1)}, u32[]{:S(2)}, u32[]{:S(2)}) collective-permute-start(f32[2,16,512]{2,1,0:T(8,128)S(1)} %maximum_add_fusion.4), channel_id=1, source_target_pairs={{0,8},{8,16},{16,24},{24,32},{32,40},{40,48},{48,56},{56,64},{64,7... | collective-permute-start | bytes 196616 | tf_op jit(solution)/shard_map/while/body/eval_jaxpr/ppermute | solution.py:15
  332.5 8.3 %collective-permute-start = (f32[2,16,512]{2,1,0:T(8,128)S(1)}, f32[2,16,512]{2,1,0:T(8,128)S(1)}, u32[]{:S(2)}, u32[]{:S(2)}) collective-permute-start(f32[2,16,512]{2,1,0:T(8,128)S(1)} %maximum_add_fusion.4), channel_id=1, source_target_pairs={{0,8},{8,16},{16,24},{24,32},{32,40},{40,48},{48,56},{56,64},{64,7... | collective-permute-start | bytes 196616 | tf_op jit(solution)/shard_map/while/body/eval_jaxpr/ppermute | solution.py:15
  340.9 8.6 %collective-permute-start = (f32[2,16,512]{2,1,0:T(8,128)S(1)}, f32[2,16,512]{2,1,0:T(8,128)S(1)}, u32[]{:S(2)}, u32[]{:S(2)}) collective-permute-start(f32[2,16,512]{2,1,0:T(8,128)S(1)} %maximum_add_fusion.4), channel_id=1, source_target_pairs={{0,8},{8,16},{16,24},{24,32},{32,40},{40,48},{48,56},{56,64},{64,7... | collective-permute-start | bytes 196616 | tf_op jit(solution)/shard_map/while/body/eval_jaxpr/ppermute | solution.py:15
  349.4 8.3 %collective-permute-start = (f32[2,16,512]{2,1,0:T(8,128)S(1)}, f32[2,16,512]{2,1,0:T(8,128)S(1)}, u32[]{:S(2)}, u32[]{:S(2)}) collective-permute-start(f32[2,16,512]{2,1,0:T(8,128)S(1)} %maximum_add_fusion.4), channel_id=1, source_target_pairs={{0,8},{8,16},{16,24},{24,32},{32,40},{40,48},{48,56},{56,64},{64,7... | collective-permute-start | bytes 196616 | tf_op jit(solution)/shard_map/while/body/eval_jaxpr/ppermute | solution.py:15
  357.7 8.3 %collective-permute-start = (f32[2,16,512]{2,1,0:T(8,128)S(1)}, f32[2,16,512]{2,1,0:T(8,128)S(1)}, u32[]{:S(2)}, u32[]{:S(2)}) collective-permute-start(f32[2,16,512]{2,1,0:T(8,128)S(1)} %maximum_add_fusion.4), channel_id=1, source_target_pairs={{0,8},{8,16},{16,24},{24,32},{32,40},{40,48},{48,56},{56,64},{64,7... | collective-permute-start | bytes 196616 | tf_op jit(solution)/shard_map/while/body/eval_jaxpr/ppermute | solution.py:15
  366.1 8.3 %collective-permute-start = (f32[2,16,512]{2,1,0:T(8,128)S(1)}, f32[2,16,512]{2,1,0:T(8,128)S(1)}, u32[]{:S(2)}, u32[]{:S(2)}) collective-permute-start(f32[2,16,512]{2,1,0:T(8,128)S(1)} %maximum_add_fusion.4), channel_id=1, source_target_pairs={{0,8},{8,16},{16,24},{24,32},{32,40},{40,48},{48,56},{56,64},{64,7... | collective-permute-start | bytes 196616 | tf_op jit(solution)/shard_map/while/body/eval_jaxpr/ppermute | solution.py:15
  374.4 8.3 %collective-permute-start = (f32[2,16,512]{2,1,0:T(8,128)S(1)}, f32[2,16,512]{2,1,0:T(8,128)S(1)}, u32[]{:S(2)}, u32[]{:S(2)}) collective-permute-start(f32[2,16,512]{2,1,0:T(8,128)S(1)} %maximum_add_fusion.4), channel_id=1, source_target_pairs={{0,8},{8,16},{16,24},{24,32},{32,40},{40,48},{48,56},{56,64},{64,7... | collective-permute-start | bytes 196616 | tf_op jit(solution)/shard_map/while/body/eval_jaxpr/ppermute | solution.py:15
  382.7 8.3 %collective-permute-start = (f32[2,16,512]{2,1,0:T(8,128)S(1)}, f32[2,16,512]{2,1,0:T(8,128)S(1)}, u32[]{:S(2)}, u32[]{:S(2)}) collective-permute-start(f32[2,16,512]{2,1,0:T(8,128)S(1)} %maximum_add_fusion.4), channel_id=1, source_target_pairs={{0,8},{8,16},{16,24},{24,32},{32,40},{40,48},{48,56},{56,64},{64,7... | collective-permute-start | bytes 196616 | tf_op jit(solution)/shard_map/while/body/eval_jaxpr/ppermute | solution.py:15
  391.0 8.3 %collective-permute-start = (f32[2,16,512]{2,1,0:T(8,128)S(1)}, f32[2,16,512]{2,1,0:T(8,128)S(1)}, u32[]{:S(2)}, u32[]{:S(2)}) collective-permute-start(f32[2,16,512]{2,1,0:T(8,128)S(1)} %maximum_add_fusion.4), channel_id=1, source_target_pairs={{0,8},{8,16},{16,24},{24,32},{32,40},{40,48},{48,56},{56,64},{64,7... | collective-permute-start | bytes 196616 | tf_op jit(solution)/shard_map/while/body/eval_jaxpr/ppermute | solution.py:15
  449.7 29.4 %copy-start.5 = (f32[512]{0:T(512)S(1)}, f32[512]{0:T(512)}, u32[]{:S(2)}) copy-start(f32[512]{0:T(512)} %param.20) | copy-start | bytes 6148
  449.7 29.6 %copy-start.4 = (bf16[256,512]{1,0:T(8,128)(2,1)S(1)}, bf16[256,512]{1,0:T(8,128)(2,1)}, u32[]{:S(2)}) copy-start(bf16[256,512]{1,0:T(8,128)(2,1)} %param.13) | copy-start | bytes 786436
Sparse Core Ops, SparseCore 0:
  484.4 71.2 reduce-scatter.1
where the time goes:
time: 572 us; the launch traced here: 563 us
  waiting for transfers between devices  268 us (47%)
  matrix products  107 us (19%)
  starting transfers between devices  61 us (11%)
  local copies, waits for them, and re-layouts  60.6 us (11%)
  other arithmetic  51.3 us (9%)
  between operations  13.8 us (2%)
    ppermute x31, waiting for transfers between devices, passed_along(): lax.ppermute(value, axis, [(source, source + steps) for source in range(f...  197 us
    reduce_scatter x1, waiting for transfers between devices, per_device(): lax.psum_scatter(lax.dot_general(out_weight, gated_out, (((1,), (1,)), ((...  71.4 us
    dot_general x1, matrix products, per_device(): jnp.einsum('kjmc,bjc->kbmc', powers_table[:, ::-1], blocked, precision=PR...  62.8 us
    ppermute x31, starting transfers between devices, passed_along(): lax.ppermute(value, axis, [(source, source + steps) for source in range(f...  61 us
    sub x1, other arithmetic, per_device(): residue_real * ahead_pow[0] - residue_imag * ahead_pow[1]  34.9 us
    gather x2, local copies, waits for them, and re-layouts, per_device(): response[jnp.clip(lag_index, 0, BLOCK - 1)]  33.2 us
    dot_general x1, matrix products, per_device(): jnp.einsum('tsc,bsc->btc', toeplitz, blocked, precision=PRECISE)  29 us
    rev x1, local copies, waits for them, and re-layouts, per_device(): powers_table[:, ::-1]  13.5 us
  transfers between devices with their start and end apart: 32, of which 32 were waited for; matrix products, arithmetic and copies ran while one was open for 0% of the time, Pallas kernels for 0%

commit v1 on v0

v1 whole, which is shorter than its diff:
```python
import functools

import jax
import jax.numpy as jnp
from jax import lax
from jax.experimental import pallas as pl
from jax.experimental.pallas import tpu as pltpu
from jax.sharding import PartitionSpec as P

MESH = pl.DeviceIdType.MESH
MODES = 16
STATE = 2 * MODES
LANES = 128
BLOCKS = 8
NX = 4
NY = 4
GROUPS = 2


def cmul(ar, ai, br, bi):
    return ar * br - ai * bi, ar * bi + ai * br


def advanced(step, state):
    real, imag = cmul(step[:MODES], step[MODES:], state[:MODES], state[MODES:])
    return jnp.concatenate([real, imag], axis=0)


def kernel(
    nz,
    gate,
    key,
    value,
    decay,
    angle,
    res_real,
    res_imag,
    skip,
    weight,
    out,
    gate_v,
    key_v,
    value_v,
    decay_v,
    angle_v,
    real_v,
    imag_v,
    skip_v,
    w_own,
    w_sib,
    u,
    g_perm,
    power,
    ker,
    taps,
    lam_block,
    lam_span,
    lam_row,
    sums,
    tot,
    tot_in,
    row_tot,
    row_in,
    before,
    start_out,
    start_in,
    states,
    local,
    g_own,
    g_sib,
    far_out,
    far_in,
    up_out,
    up_in,
    down_out,
    down_in,
    up_part,
    down_part,
    own_part,
    final,
    load_sem,
    wsib_sem,
    tot_send,
    tot_recv,
    row_send,
    row_recv,
    start_send,
    start_recv,
    gsib_send,
    gsib_recv,
    far_send,
    far_recv,
    up_send,
    up_recv,
    down_send,
    down_recv,
):
    rows, width = key_v.shape
    step = rows // BLOCKS
    quarters = width // LANES
    group_rows = rows // GROUPS
    half = group_rows // 2
    ctx, ch = lax.axis_index("ctx"), lax.axis_index("ch")
    z, x = ctx // NX, lax.rem(ctx, NX)
    y, core = ch // 2, lax.rem(ch, 2)
    sibling = {"ctx": ctx, "ch": y * 2 + (1 - core)}
    y_up, y_down, y_far = (lax.rem(y + d, NY) for d in (1, NY - 1, 2))
    up_dev = {"ctx": ctx, "ch": y_up * 2 + core}
    down_dev = {"ctx": ctx, "ch": y_down * 2 + core}

    def remote(src, dst, send, recv, device):
        return pltpu.make_async_remote_copy(
            src_ref=src, dst_ref=dst, send_sem=send, recv_sem=recv, device_id=device, device_id_type=MESH
        )

    pairs = (
        (decay, decay_v),
        (angle, angle_v),
        (key, key_v),
        (value, value_v),
        (res_real, real_v),
        (res_imag, imag_v),
        (skip, skip_v),
        (gate, gate_v),
        (weight.at[:, core], w_own),
    )
    loads = [pltpu.make_async_copy(src, dst, load_sem.at[i]) for i, (src, dst) in enumerate(pairs)]
    for load in loads:
        load.start()

    barrier = pltpu.get_barrier_semaphore()
    peers = [sibling, up_dev, down_dev]
    peers += [{"ctx": z * NX + lax.rem(x + d, NX), "ch": ch} for d in range(1, NX)]
    peers += [{"ctx": lax.rem(z + d, nz) * NX + x, "ch": ch} for d in range(1, nz)]
    for peer in peers:
        pl.semaphore_signal(barrier, inc=1, device_id=peer, device_id_type=MESH)

    loads[0].wait()
    loads[1].wait()
    magnitude = jnp.exp(-decay_v[...])
    lam_r = magnitude * jnp.cos(angle_v[...])
    lam_i = magnitude * jnp.sin(angle_v[...])

    def lanes(q):
        return slice(q * LANES, (q + 1) * LANES)

    def store_power(j, carry):
        pr, pi = carry
        for q in range(quarters):
            power[q, j, :MODES, :] = pr[:, lanes(q)]
            power[q, j, MODES:, :] = pi[:, lanes(q)]
        return cmul(pr, pi, lam_r, lam_i)

    pr, pi = lax.fori_loop(0, step, store_power, (jnp.ones_like(lam_r), jnp.zeros_like(lam_r)))
    for q in range(quarters):
        power[q, step, :MODES, :] = pr[:, lanes(q)]
        power[q, step, MODES:, :] = pi[:, lanes(q)]
        lam_block[q, :MODES, :] = pr[:, lanes(q)]
        lam_block[q, MODES:, :] = pi[:, lanes(q)]
    for _ in range(3):
        pr, pi = cmul(pr, pi, pr, pi)
    for q in range(quarters):
        lam_span[q, :MODES, :] = pr[:, lanes(q)]
        lam_span[q, MODES:, :] = pi[:, lanes(q)]
    for _ in range(2):
        pr, pi = cmul(pr, pi, pr, pi)
    for q in range(quarters):
        lam_row[q, :MODES, :] = pr[:, lanes(q)]
        lam_row[q, MODES:, :] = pi[:, lanes(q)]

    loads[2].wait()
    loads[3].wait()
    for q in range(quarters):
        u[q, : 8 * BLOCKS, :] = jnp.zeros((8 * BLOCKS, LANES), jnp.float32)
        for b in range(BLOCKS):
            part = slice(b * step, (b + 1) * step)
            drive = key_v[part, lanes(q)].astype(jnp.float32) * value_v[part, lanes(q)].astype(jnp.float32)
            u[q, pl.ds(8 * BLOCKS + b, step, stride=BLOCKS), :] = drive

    pl.semaphore_wait(barrier, len(peers))
    w_copy = remote(weight.at[:, 1 - core], w_sib, wsib_sem.at[0], wsib_sem.at[1], sibling)
    w_copy.start()

    def total_of(i, _):
        q = lax.rem(x + 1 + i, NX)

        def add_token(j, acc):
            row = u[q, pl.ds(pl.multiple_of(8 * BLOCKS + j * BLOCKS, BLOCKS), BLOCKS), :]
            return tuple(acc[k] + power[q, step - 1 - j, pl.ds(k, 1), :] * row for k in range(STATE))

        acc = lax.fori_loop(
            0, step, add_token, tuple(jnp.zeros((BLOCKS, LANES), jnp.float32) for _ in range(STATE)), unroll=2
        )
        for k in range(STATE):
            sums[q, pl.ds(k, BLOCKS, stride=STATE), :] = acc[k]
        lam = lam_block[q]
        state = sums[q, :STATE, :]
        for b in range(1, BLOCKS):
            state = advanced(lam, state) + sums[q, b * STATE : (b + 1) * STATE, :]
        tot[q] = state

        @pl.when(i < NX - 1)
        def _():
            remote(
                tot.at[q], tot_in.at[x], tot_send.at[q], tot_recv.at[x], {"ctx": z * NX + q, "ch": ch}
            ).start()

        @pl.when(i == NX - 1)
        def _():
            tot_in[x] = state

        return 0

    lax.fori_loop(0, quarters, total_of, 0)

    for i in (4, 5, 6):
        loads[i].wait()
    for q in range(quarters):
        rr, ri = real_v[:, lanes(q)], imag_v[:, lanes(q)]
        taps[q, 0:1, :] = jnp.sum(rr, axis=0, keepdims=True) + skip_v[:, lanes(q)]

        def store_ker(j, _, q=q, rr=rr, ri=ri):
            p = power[q, j + 1]
            kr, ki = cmul(rr, ri, p[:MODES], p[MODES:])
            ker[q, j, :MODES, :] = kr
            ker[q, j, MODES:, :] = -ki
            taps[q, pl.ds(j + 1, 1), :] = jnp.sum(kr, axis=0, keepdims=True)
            return 0

        lax.fori_loop(0, step, store_ker, 0, unroll=4)

    for d in range(1, NX):
        src = lax.rem(x + d, NX)
        remote(tot.at[src], tot_in.at[src], tot_send.at[src], tot_recv.at[src], sibling).wait_recv()
    lam = lam_span[x]
    state = tot_in[0]
    for i in range(1, NX):
        state = advanced(lam, state) + tot_in[i]
    row_tot[...] = state

    def row_copy(d):
        return remote(
            row_tot, row_in.at[z], row_send.at[d], row_recv.at[z], {"ctx": lax.rem(z + d, nz) * NX + x, "ch": ch}
        )

    for d in range(1, nz):

        @pl.when(z + d < nz)
        def _():
            row_copy(d).start()

    loads[7].wait()
    chunk = 8 * BLOCKS

    def fir(q, _):
        for c in range(step // 8):
            acc = None
            for lag in range(8 * c + 8):
                begin = chunk + c * chunk - lag * BLOCKS
                term = taps[q, pl.ds(lag, 1), :] * u[q, begin : begin + chunk, :]
                acc = term if acc is None else acc + term
            local[q, c * chunk : (c + 1) * chunk, :] = acc
        return 0

    lax.fori_loop(0, quarters, fir, 0)
    for q in range(quarters):
        for b in range(BLOCKS):
            part = slice(b * step, (b + 1) * step)
            g_perm[q, pl.ds(b, step, stride=BLOCKS), :] = gate_v[part, lanes(q)].astype(jnp.float32)

    lam = lam_row[x]
    before[...] = jnp.zeros_like(before)
    for s in range(nz - 1):

        @pl.when(s < z)
        def _():
            remote(row_tot, row_in.at[s], row_send.at[0], row_recv.at[s], sibling).wait_recv()
            before[...] = advanced(lam, before[...]) + row_in[s]

    lam = lam_span[x]
    state = before[...]
    for i in range(NX):
        start_out[i] = state
        if i < NX - 1:
            state = advanced(lam, state) + tot_in[i]
    for d in range(1, NX):
        to = lax.rem(x + d, NX)
        remote(
            start_out.at[to], start_in.at[x], start_send.at[d], start_recv.at[x], {"ctx": z * NX + to, "ch": ch}
        ).start()
    start_in[x] = start_out[x]
    for d in range(1, NX):
        src = lax.rem(x + d, NX)
        remote(start_out.at[src], start_in.at[src], start_send.at[0], start_recv.at[src], sibling).wait_recv()

    for q in range(quarters):
        lam = lam_block[q]
        state = start_in[q]
        for b in range(BLOCKS):
            states[q, pl.ds(b, STATE, stride=BLOCKS), :] = state
            if b < BLOCKS - 1:
                state = advanced(lam, state) + sums[q, b * STATE : (b + 1) * STATE, :]

    def rows_of(g):
        return slice(g * group_rows, (g + 1) * group_rows)

    def gated(g):
        pairs_in_group = group_rows // (2 * BLOCKS)

        for q in range(quarters):
            held = [states[q, k * BLOCKS : (k + 1) * BLOCKS, :] for k in range(STATE)]

            def two_tokens(i, _, q=q, held=held):
                done = []
                for t in range(2):
                    j = 2 * i + t
                    at = pl.ds(pl.multiple_of(j * BLOCKS, BLOCKS), BLOCKS)
                    partial = [local[q, at, :], None, None, None]
                    for k in range(STATE):
                        term = ker[q, j, pl.ds(k, 1), :] * held[k]
                        partial[k % 4] = term if partial[k % 4] is None else partial[k % 4] + term
                    total = (partial[0] + partial[1]) + (partial[2] + partial[3])
                    done.append(total * g_perm[q, at, :])
                to = pl.ds(pl.multiple_of(i * 2 * BLOCKS, 2 * BLOCKS), 2 * BLOCKS)
                g_own[to, lanes(q)] = jnp.concatenate(done, axis=0).astype(jnp.bfloat16)
                return 0

            lax.fori_loop(g * pairs_in_group, (g + 1) * pairs_in_group, two_tokens, 0)

    def sib_copy(g):
        at = rows_of(g)
        return remote(g_own.at[at], g_sib.at[at], gsib_send.at[g], gsib_recv.at[g], sibling)

    def product(g, to):
        dims = (((1,), (1,)), ((), ()))
        mine = lax.dot_general(g_own[rows_of(g), :], w_own[to], dims, preferred_element_type=jnp.float32)
        theirs = lax.dot_general(g_sib[rows_of(g), :], w_sib[to], dims, preferred_element_type=jnp.float32)
        return mine + theirs

    low, high = slice(0, half), slice(half, group_rows)

    def far_copies(g):
        return (
            remote(far_out.at[g, low], far_in.at[g, low], far_send.at[g, 0], far_recv.at[g, 0], up_dev),
            remote(far_out.at[g, high], far_in.at[g, high], far_send.at[g, 1], far_recv.at[g, 1], down_dev),
        )

    def up_copy(g, i):
        at = (low, high)[i]
        return remote(up_out.at[g, at], up_in.at[g, at], up_send.at[g, i], up_recv.at[g, i], up_dev)

    def down_copy(g, i):
        at = (low, high)[i]
        return remote(down_out.at[g, at], down_in.at[g, at], down_send.at[g, i], down_recv.at[g, i], down_dev)

    def send_off(g):
        far_out[g] = product(g, y_far).astype(jnp.bfloat16)
        for copy in far_copies(g):
            copy.start()
        part = product(g, y_up)
        up_out[g, high] = part[half:].astype(jnp.bfloat16)
        up_copy(g, 1).start()
        up_part[...] = part[:half]
        part = product(g, y_down)
        down_out[g, low] = part[:half].astype(jnp.bfloat16)
        down_copy(g, 0).start()
        down_part[...] = part[half:]

    def send_rest(g):
        arrived = far_copies(g)
        arrived[0].wait_recv()
        up_out[g, low] = (up_part[...] + far_in[g, low].astype(jnp.float32)).astype(jnp.bfloat16)
        up_copy(g, 0).start()
        arrived[1].wait_recv()
        down_out[g, high] = (down_part[...] + far_in[g, high].astype(jnp.float32)).astype(jnp.bfloat16)
        down_copy(g, 1).start()
        own_part[rows_of(g), :] = product(g, y)

    for g in range(GROUPS):
        gated(g)
        sib_copy(g).start()
        if g == 0:
            loads[8].wait()
            w_copy.wait_recv()
        else:
            send_rest(g - 1)
        sib_copy(g).wait_recv()
        send_off(g)
    send_rest(GROUPS - 1)

    for g in range(GROUPS):
        for i in (1, 0):
            at = (low, high)[i]
            down_copy(g, 1 - i).wait_recv()
            up_copy(g, i).wait_recv()
        whole = own_part[rows_of(g), :] + up_in[g].astype(jnp.float32) + down_in[g].astype(jnp.float32)
        for q in range(quarters):
            final[q, rows_of(g), :] = whole[:, lanes(q)]
    for q in range(quarters):
        for b in range(BLOCKS):
            out[b * step : (b + 1) * step, lanes(q)] = final[q, pl.ds(b, step, stride=BLOCKS), :].astype(jnp.bfloat16)

    w_copy.wait_send()
    for d in range(1, NX):
        q = lax.rem(x + d, NX)
        remote(tot.at[q], tot_in.at[x], tot_send.at[q], tot_recv.at[x], sibling).wait_send()
        remote(start_out.at[q], start_in.at[x], start_send.at[d], start_recv.at[x], sibling).wait_send()
    for d in range(1, nz):

        @pl.when(z + d < nz)
        def _():
            row_copy(d).wait_send()

    for g in range(GROUPS):
        sib_copy(g).wait_send()
        for copy in far_copies(g):
            copy.wait_send()
        for i in range(2):
            up_copy(g, i).wait_send()
            down_copy(g, i).wait_send()


def per_device(
    gate_signal, key_signal, value_signal, pole_decay, pole_angle, residue_real, residue_imag, skip_gain, out_weight
):
    rows, width = key_signal.shape
    nz = lax.axis_size("ctx") // NX
    quarters = width // LANES
    step = rows // BLOCKS
    group_rows = rows // GROUPS
    outs = out_weight.shape[0] // (2 * NY)
    weight = out_weight.reshape(NY, 2, outs, width)
    f32, bf16 = jnp.float32, jnp.bfloat16
    dma = pltpu.SemaphoreType.DMA

    def vmem(dtype, *shape):
        return pltpu.VMEM(shape, dtype)

    scratch = [
        vmem(bf16, rows, width),
        vmem(bf16, rows, width),
        vmem(bf16, rows, width),
        vmem(f32, MODES, width),
        vmem(f32, MODES, width),
        vmem(f32, MODES, width),
        vmem(f32, MODES, width),
        vmem(f32, 1, width),
        vmem(bf16, NY, outs, width),
        vmem(bf16, NY, outs, width),
        vmem(f32, quarters, 8 * BLOCKS + rows, LANES),
        vmem(f32, quarters, rows, LANES),
        vmem(f32, quarters, step + 1, STATE, LANES),
        vmem(f32, quarters, step, STATE, LANES),
        vmem(f32, quarters, step + 8, LANES),
        vmem(f32, quarters, STATE, LANES),
        vmem(f32, quarters, STATE, LANES),
        vmem(f32, quarters, STATE, LANES),
        vmem(f32, quarters, STATE * BLOCKS, LANES),
        vmem(f32, quarters, STATE, LANES),
        vmem(f32, NX, STATE, LANES),
        vmem(f32, STATE, LANES),
        vmem(f32, nz, STATE, LANES),
        vmem(f32, STATE, LANES),
        vmem(f32, NX, STATE, LANES),
        vmem(f32, NX, STATE, LANES),
        vmem(f32, quarters, STATE * BLOCKS, LANES),
        vmem(f32, quarters, rows, LANES),
        vmem(bf16, rows, width),
        vmem(bf16, rows, width),
        vmem(bf16, GROUPS, group_rows, outs),
        vmem(bf16, GROUPS, group_rows, outs),
        vmem(bf16, GROUPS, group_rows, outs),
        vmem(bf16, GROUPS, group_rows, outs),
        vmem(bf16, GROUPS, group_rows, outs),
        vmem(bf16, GROUPS, group_rows, outs),
        vmem(f32, group_rows // 2, outs),
        vmem(f32, group_rows // 2, outs),
        vmem(f32, rows, outs),
        vmem(f32, outs // LANES, rows, LANES),
        dma((9,)),
        dma((2,)),
        dma((NX,)),
        dma((NX,)),
        dma((nz,)),
        dma((nz,)),
        dma((NX,)),
        dma((NX,)),
        dma((GROUPS,)),
        dma((GROUPS,)),
        dma((GROUPS, 2)),
        dma((GROUPS, 2)),
        dma((GROUPS, 2)),
        dma((GROUPS, 2)),
        dma((GROUPS, 2)),
        dma((GROUPS, 2)),
    ]
    hbm = pl.BlockSpec(memory_space=pl.ANY)
    return pl.pallas_call(
        functools.partial(kernel, nz),
        out_shape=jax.ShapeDtypeStruct((rows, outs), bf16),
        in_specs=[hbm] * 9,
        out_specs=pl.BlockSpec(memory_space=pltpu.VMEM),
        scratch_shapes=scratch,
        compiler_params=pltpu.CompilerParams(
            collective_id=0, has_side_effects=True, vmem_limit_bytes=40 * 1024 * 1024
        ),
    )(
        gate_signal,
        key_signal,
        value_signal,
        pole_decay,
        pole_angle,
        residue_real,
        residue_imag,
        skip_gain.reshape(1, width),
        weight,
    )


def solution(mesh):
    return jax.shard_map(
        per_device,
        mesh=mesh,
        in_specs=(
            P("ctx", "ch"),
            P("ctx", "ch"),
            P("ctx", "ch"),
            P(None, "ch"),
            P(None, "ch"),
            P(None, "ch"),
            P(None, "ch"),
            P("ch"),
            P(None, "ch"),
        ),
        out_specs=P("ctx", "ch"),
        check_vma=False,
    )
```

time: 572 us -> 45.4 us (0.08)
  the two profiles are of different devices: /device:TPU:224 before, /device:TPU:33 now
where the time goes in v1:
time: 45.4 us; the launch traced here: 44.9 us
  Pallas kernels  35.4 us (78%)
  local copies, waits for them, and re-layouts  9.45 us (21%)
    pallas_call x1, Pallas kernels, per_device(): pl.pallas_call(functools.partial(kernel, nz), out_shape=jax.ShapeDtypeStr...  35.4 us
    unnamed x19, local copies, waits for them, and re-layouts  9.45 us

profile of v1, /device:TPU:33, one launch (start us, length us, event | category | flops | bytes accessed | tf_op | source)
XLA Modules:
  0.0 44.9 jit_solution(6650620542578471841)
XLA Ops:
  0.0 0.0 copy-start
  0.0 2.2 %copy-done = bf16[4096,512]{1,0:T(8,128)(2,1)S(1)} copy-done((bf16[4096,512]{1,0:T(8,128)(2,1)S(1)}, bf16[4096,512]{1,0:T(8,128)(2,1)}, u32[]{:S(2)}) %copy-start) | copy-done | bytes 4194328
  2.2 0.0 copy-start.1
  2.2 0.9 %copy-done.1 = bf16[256,512]{1,0:T(8,128)(2,1)S(1)} copy-done((bf16[256,512]{1,0:T(8,128)(2,1)S(1)}, bf16[256,512]{1,0:T(8,128)(2,1)}, u32[]{:S(2)}) %copy-start.1) | copy-done | bytes 262168
  3.1 0.0 copy-start.2
  3.1 0.9 %copy-done.2 = bf16[256,512]{1,0:T(8,128)(2,1)S(1)} copy-done((bf16[256,512]{1,0:T(8,128)(2,1)S(1)}, bf16[256,512]{1,0:T(8,128)(2,1)}, u32[]{:S(2)}) %copy-start.2) | copy-done | bytes 262168
  4.1 0.0 copy-start.3
  4.1 0.9 %copy-done.3 = bf16[256,512]{1,0:T(8,128)(2,1)S(1)} copy-done((bf16[256,512]{1,0:T(8,128)(2,1)S(1)}, bf16[256,512]{1,0:T(8,128)(2,1)}, u32[]{:S(2)}) %copy-start.3) | copy-done | bytes 262168
  5.0 0.0 copy-start.4
  5.0 0.8 %copy-done.4 = f32[16,512]{1,0:T(8,128)S(1)} copy-done((f32[16,512]{1,0:T(8,128)S(1)}, f32[16,512]{1,0:T(8,128)}, u32[]{:S(2)}) %copy-start.4) | copy-done | bytes 32792
  5.8 0.0 copy-start.5
  5.8 0.8 %copy-done.5 = f32[16,512]{1,0:T(8,128)S(1)} copy-done((f32[16,512]{1,0:T(8,128)S(1)}, f32[16,512]{1,0:T(8,128)}, u32[]{:S(2)}) %copy-start.5) | copy-done | bytes 32792
  6.6 0.0 copy-start.6
  6.6 0.8 %copy-done.6 = f32[16,512]{1,0:T(8,128)S(1)} copy-done((f32[16,512]{1,0:T(8,128)S(1)}, f32[16,512]{1,0:T(8,128)}, u32[]{:S(2)}) %copy-start.6) | copy-done | bytes 32792
  7.3 0.0 copy-start.7
  7.3 0.8 %copy-done.7 = f32[16,512]{1,0:T(8,128)S(1)} copy-done((f32[16,512]{1,0:T(8,128)S(1)}, f32[16,512]{1,0:T(8,128)}, u32[]{:S(2)}) %copy-start.7) | copy-done | bytes 32792
  8.1 0.0 copy-start.8
  8.1 0.7 %copy-done.8 = f32[512]{0:T(512)S(1)} copy-done((f32[512]{0:T(512)S(1)}, f32[512]{0:T(512)}, u32[]{:S(2)}) %copy-start.8) | copy-done | bytes 2072
  8.8 35.4 %shard_map.91 = bf16[256,512]{1,0:T(8,128)(2,1)S(1)} custom-call(bf16[256,512]{1,0:T(8,128)(2,1)S(1)} %copy-done.1, bf16[256,512]{1,0:T(8,128)(2,1)S(1)} %copy-done.2, bf16[256,512]{1,0:T(8,128)(2,1)S(1)} %copy-done.3, f32[16,512]{1,0:T(8,128)S(1)} %copy-done.4, f32[16,512]{1,0:T(8,128)S(1)} %copy-done.5, f32[16,512]{1,0:T(8,128)S(1)} %copy-done.6, ...), custom_call_target="tpu_custom_call" | custom-call | tf_op jit(solution)/shard_map/pallas_call | solution.py:498
  44.2 0.7 %copy.11 = bf16[256,512]{1,0:T(8,128)(2,1)} copy(bf16[256,512]{1,0:T(8,128)(2,1)S(1)} %shard_map.91) | data formatting | bytes 524288
Async XLA Ops:
  0.0 2.2 %copy-start = (bf16[4096,512]{1,0:T(8,128)(2,1)S(1)}, bf16[4096,512]{1,0:T(8,128)(2,1)}, u32[]{:S(2)}) copy-start(bf16[4096,512]{1,0:T(8,128)(2,1)} %param.17) | copy-start | bytes 12582916
  2.2 0.9 %copy-start.1 = (bf16[256,512]{1,0:T(8,128)(2,1)S(1)}, bf16[256,512]{1,0:T(8,128)(2,1)}, u32[]{:S(2)}) copy-start(bf16[256,512]{1,0:T(8,128)(2,1)} %gate.1) | copy-start | bytes 786436
  3.1 0.9 %copy-start.2 = (bf16[256,512]{1,0:T(8,128)(2,1)S(1)}, bf16[256,512]{1,0:T(8,128)(2,1)}, u32[]{:S(2)}) copy-start(bf16[256,512]{1,0:T(8,128)(2,1)} %key.1) | copy-start | bytes 786436
  4.1 0.9 %copy-start.3 = (bf16[256,512]{1,0:T(8,128)(2,1)S(1)}, bf16[256,512]{1,0:T(8,128)(2,1)}, u32[]{:S(2)}) copy-start(bf16[256,512]{1,0:T(8,128)(2,1)} %value.1) | copy-start | bytes 786436
  5.0 0.8 %copy-start.4 = (f32[16,512]{1,0:T(8,128)S(1)}, f32[16,512]{1,0:T(8,128)}, u32[]{:S(2)}) copy-start(f32[16,512]{1,0:T(8,128)} %decay.1) | copy-start | bytes 98308
  5.8 0.8 %copy-start.5 = (f32[16,512]{1,0:T(8,128)S(1)}, f32[16,512]{1,0:T(8,128)}, u32[]{:S(2)}) copy-start(f32[16,512]{1,0:T(8,128)} %angle.1) | copy-start | bytes 98308
  6.6 0.8 %copy-start.6 = (f32[16,512]{1,0:T(8,128)S(1)}, f32[16,512]{1,0:T(8,128)}, u32[]{:S(2)}) copy-start(f32[16,512]{1,0:T(8,128)} %res_real.1) | copy-start | bytes 98308
  7.3 0.8 %copy-start.7 = (f32[16,512]{1,0:T(8,128)S(1)}, f32[16,512]{1,0:T(8,128)}, u32[]{:S(2)}) copy-start(f32[16,512]{1,0:T(8,128)} %res_imag.1) | copy-start | bytes 98308
  8.1 0.7 %copy-start.8 = (f32[512]{0:T(512)S(1)}, f32[512]{0:T(512)}, u32[]{:S(2)}) copy-start(f32[512]{0:T(512)} %param.16) | copy-start | bytes 6148

commit v2 on v1

--- a/solution.py
+++ b/solution.py
@@ -14,7 +14,8 @@
 BLOCKS = 8
 NX = 4
 NY = 4
-GROUPS = 2
+GROUP_ROWS = (64, 192)
+GROUPS = len(GROUP_ROWS)
 
 
 def cmul(ar, ai, br, bi):
@@ -46,8 +47,7 @@
     real_v,
     imag_v,
     skip_v,
-    w_own,
-    w_sib,
+    w_all,
     u,
     g_perm,
     power,
@@ -66,8 +66,7 @@
     start_in,
     states,
     local,
-    g_own,
-    g_sib,
+    g_all,
     far_out,
     far_in,
     up_out,
@@ -98,8 +97,6 @@
     rows, width = key_v.shape
     step = rows // BLOCKS
     quarters = width // LANES
-    group_rows = rows // GROUPS
-    half = group_rows // 2
     ctx, ch = lax.axis_index("ctx"), lax.axis_index("ch")
     z, x = ctx // NX, lax.rem(ctx, NX)
     y, core = ch // 2, lax.rem(ch, 2)
@@ -122,7 +119,7 @@
         (res_imag, imag_v),
         (skip, skip_v),
         (gate, gate_v),
-        (weight.at[:, core], w_own),
+        (weight.at[:, core], w_all.at[:, :, :width]),
     )
     loads = [pltpu.make_async_copy(src, dst, load_sem.at[i]) for i, (src, dst) in enumerate(pairs)]
     for load in loads:
@@ -177,12 +174,10 @@
             drive = key_v[part, lanes(q)].astype(jnp.float32) * value_v[part, lanes(q)].astype(jnp.float32)
             u[q, pl.ds(8 * BLOCKS + b, step, stride=BLOCKS), :] = drive
 
-    pl.semaphore_wait(barrier, len(peers))
-    w_copy = remote(weight.at[:, 1 - core], w_sib, wsib_sem.at[0], wsib_sem.at[1], sibling)
-    w_copy.start()
+    w_copy = remote(weight.at[:, 1 - core], w_all.at[:, :, width:], wsib_sem.at[0], wsib_sem.at[1], sibling)
 
     def total_of(i, _):
-        q = lax.rem(x + 1 + i, NX)
+        q = lax.rem(x + jnp.where(i == 0, 2, jnp.where(i == 1, 1, jnp.where(i == 2, 3, 0))), NX)
 
         def add_token(j, acc):
             row = u[q, pl.ds(pl.multiple_of(8 * BLOCKS + j * BLOCKS, BLOCKS), BLOCKS), :]
@@ -199,6 +194,10 @@
             state = advanced(lam, state) + sums[q, b * STATE : (b + 1) * STATE, :]
         tot[q] = state
 
+        @pl.when(i == 0)
+        def _():
+            pl.semaphore_wait(barrier, len(peers))
+
         @pl.when(i < NX - 1)
         def _():
             remote(
@@ -212,6 +211,7 @@
         return 0
 
     lax.fori_loop(0, quarters, total_of, 0)
+    w_copy.start()
 
     for i in (4, 5, 6):
         loads[i].wait()
@@ -243,7 +243,7 @@
             row_tot, row_in.at[z], row_send.at[d], row_recv.at[z], {"ctx": lax.rem(z + d, nz) * NX + x, "ch": ch}
         )
 
-    for d in range(1, nz):
+    for d in reversed(range(1, nz)):
 
         @pl.when(z + d < nz)
         def _():
@@ -283,7 +283,7 @@
         start_out[i] = state
         if i < NX - 1:
             state = advanced(lam, state) + tot_in[i]
-    for d in range(1, NX):
+    for d in (2, 1, 3):
         to = lax.rem(x + d, NX)
         remote(
             start_out.at[to], start_in.at[x], start_send.at[d], start_recv.at[x], {"ctx": z * NX + to, "ch": ch}
@@ -302,10 +302,16 @@
                 state = advanced(lam, state) + sums[q, b * STATE : (b + 1) * STATE, :]
 
     def rows_of(g):
-        return slice(g * group_rows, (g + 1) * group_rows)
+        begin = sum(GROUP_ROWS[:g])
+        return slice(begin, begin + GROUP_ROWS[g])
+
+    def halves_of(g):
+        at = rows_of(g)
+        middle = (at.start + at.stop) // 2
+        return slice(at.start, middle), slice(middle, at.stop)
 
     def gated(g):
-        pairs_in_group = group_rows // (2 * BLOCKS)
+        at_rows = rows_of(g)
 
         for q in range(quarters):
             held = [states[q, k * BLOCKS : (k + 1) * BLOCKS, :] for k in range(STATE)]
@@ -322,80 +328,83 @@
                     total = (partial[0] + partial[1]) + (partial[2] + partial[3])
                     done.append(total * g_perm[q, at, :])
                 to = pl.ds(pl.multiple_of(i * 2 * BLOCKS, 2 * BLOCKS), 2 * BLOCKS)
-                g_own[to, lanes(q)] = jnp.concatenate(done, axis=0).astype(jnp.bfloat16)
+                g_all[to, lanes(q)] = jnp.concatenate(done, axis=0).astype(jnp.bfloat16)
                 return 0
 
-            lax.fori_loop(g * pairs_in_group, (g + 1) * pairs_in_group, two_tokens, 0)
+            lax.fori_loop(at_rows.start // (2 * BLOCKS), at_rows.stop // (2 * BLOCKS), two_tokens, 0)
 
     def sib_copy(g):
         at = rows_of(g)
-        return remote(g_own.at[at], g_sib.at[at], gsib_send.at[g], gsib_recv.at[g], sibling)
+        return remote(g_all.at[at, :width], g_all.at[at, width:], gsib_send.at[g], gsib_recv.at[g], sibling)
 
     def product(g, to):
-        dims = (((1,), (1,)), ((), ()))
-        mine = lax.dot_general(g_own[rows_of(g), :], w_own[to], dims, preferred_element_type=jnp.float32)
-        theirs = lax.dot_general(g_sib[rows_of(g), :], w_sib[to], dims, preferred_element_type=jnp.float32)
-        return mine + theirs
-
-    low, high = slice(0, half), slice(half, group_rows)
+        return lax.dot_general(
+            g_all[rows_of(g), :], w_all[to], (((1,), (1,)), ((), ())), preferred_element_type=jnp.float32
+        )
 
     def far_copies(g):
+        low, high = halves_of(g)
         return (
-            remote(far_out.at[g, low], far_in.at[g, low], far_send.at[g, 0], far_recv.at[g, 0], up_dev),
-            remote(far_out.at[g, high], far_in.at[g, high], far_send.at[g, 1], far_recv.at[g, 1], down_dev),
+            remote(far_out.at[low], far_in.at[low], far_send.at[g, 0], far_recv.at[g, 0], up_dev),
+            remote(far_out.at[high], far_in.at[high], far_send.at[g, 1], far_recv.at[g, 1], down_dev),
         )
 
     def up_copy(g, i):
-        at = (low, high)[i]
-        return remote(up_out.at[g, at], up_in.at[g, at], up_send.at[g, i], up_recv.at[g, i], up_dev)
+        at = halves_of(g)[i]
+        return remote(up_out.at[at], up_in.at[at], up_send.at[g, i], up_recv.at[g, i], up_dev)
 
     def down_copy(g, i):
-        at = (low, high)[i]
-        return remote(down_out.at[g, at], down_in.at[g, at], down_send.at[g, i], down_recv.at[g, i], down_dev)
+        at = halves_of(g)[i]
+        return remote(down_out.at[at], down_in.at[at], down_send.at[g, i], down_recv.at[g, i], down_dev)
 
     def send_off(g):
-        far_out[g] = product(g, y_far).astype(jnp.bfloat16)
+        low, high = halves_of(g)
+        half = GROUP_ROWS[g] // 2
+        far_out[rows_of(g), :] = product(g, y_far).astype(jnp.bfloat16)
         for copy in far_copies(g):
             copy.start()
         part = product(g, y_up)
-        up_out[g, high] = part[half:].astype(jnp.bfloat16)
+        up_out[high, :] = part[half:].astype(jnp.bfloat16)
         up_copy(g, 1).start()
-        up_part[...] = part[:half]
+        up_part[low, :] = part[:half]
         part = product(g, y_down)
-        down_out[g, low] = part[:half].astype(jnp.bfloat16)
+        down_out[low, :] = part[:half].astype(jnp.bfloat16)
         down_copy(g, 0).start()
-        down_part[...] = part[half:]
+        down_part[high, :] = part[half:]
 
     def send_rest(g):
+        low, high = halves_of(g)
         arrived = far_copies(g)
         arrived[0].wait_recv()
-        up_out[g, low] = (up_part[...] + far_in[g, low].astype(jnp.float32)).astype(jnp.bfloat16)
+        up_out[low, :] = (up_part[low, :] + far_in[low, :].astype(jnp.float32)).astype(jnp.bfloat16)
         up_copy(g, 0).start()
         arrived[1].wait_recv()
-        down_out[g, high] = (down_part[...] + far_in[g, high].astype(jnp.float32)).astype(jnp.bfloat16)
+        down_out[high, :] = (down_part[high, :] + far_in[high, :].astype(jnp.float32)).astype(jnp.bfloat16)
         down_copy(g, 1).start()
         own_part[rows_of(g), :] = product(g, y)
 
-    for g in range(GROUPS):
-        gated(g)
-        sib_copy(g).start()
+    for g in range(GROUPS + 1):
+        if g < GROUPS:
+            gated(g)
+            sib_copy(g).start()
         if g == 0:
             loads[8].wait()
             w_copy.wait_recv()
-        else:
-            send_rest(g - 1)
-        sib_copy(g).wait_recv()
-        send_off(g)
+        if g > 0:
+            sib_copy(g - 1).wait_recv()
+            send_off(g - 1)
+        if g > 1:
+            send_rest(g - 2)
     send_rest(GROUPS - 1)
 
     for g in range(GROUPS):
         for i in (1, 0):
-            at = (low, high)[i]
             down_copy(g, 1 - i).wait_recv()
             up_copy(g, i).wait_recv()
-        whole = own_part[rows_of(g), :] + up_in[g].astype(jnp.float32) + down_in[g].astype(jnp.float32)
+        at = rows_of(g)
+        whole = own_part[at, :] + up_in[at, :].astype(jnp.float32) + down_in[at, :].astype(jnp.float32)
         for q in range(quarters):
-            final[q, rows_of(g), :] = whole[:, lanes(q)]
+            final[q, at, :] = whole[:, lanes(q)]
     for q in range(quarters):
         for b in range(BLOCKS):
             out[b * step : (b + 1) * step, lanes(q)] = final[q, pl.ds(b, step, stride=BLOCKS), :].astype(jnp.bfloat16)
@@ -427,7 +436,6 @@
     nz = lax.axis_size("ctx") // NX
     quarters = width // LANES
     step = rows // BLOCKS
-    group_rows = rows // GROUPS
     outs = out_weight.shape[0] // (2 * NY)
     weight = out_weight.reshape(NY, 2, outs, width)
     f32, bf16 = jnp.float32, jnp.bfloat16
@@ -445,8 +453,7 @@
         vmem(f32, MODES, width),
         vmem(f32, MODES, width),
         vmem(f32, 1, width),
-        vmem(bf16, NY, outs, width),
-        vmem(bf16, NY, outs, width),
+        vmem(bf16, NY, outs, 2 * width),
         vmem(f32, quarters, 8 * BLOCKS + rows, LANES),
         vmem(f32, quarters, rows, LANES),
         vmem(f32, quarters, step + 1, STATE, LANES),
@@ -465,16 +472,15 @@
         vmem(f32, NX, STATE, LANES),
         vmem(f32, quarters, STATE * BLOCKS, LANES),
         vmem(f32, quarters, rows, LANES),
-        vmem(bf16, rows, width),
-        vmem(bf16, rows, width),
-        vmem(bf16, GROUPS, group_rows, outs),
-        vmem(bf16, GROUPS, group_rows, outs),
-        vmem(bf16, GROUPS, group_rows, outs),
-        vmem(bf16, GROUPS, group_rows, outs),
-        vmem(bf16, GROUPS, group_rows, outs),
-        vmem(bf16, GROUPS, group_rows, outs),
-        vmem(f32, group_rows // 2, outs),
-        vmem(f32, group_rows // 2, outs),
+        vmem(bf16, rows, 2 * width),
+        vmem(bf16, rows, outs),
+        vmem(bf16, rows, outs),
+        vmem(bf16, rows, outs),
+        vmem(bf16, rows, outs),
+        vmem(bf16, rows, outs),
+        vmem(bf16, rows, outs),
+        vmem(f32, rows, outs),
+        vmem(f32, rows, outs),
         vmem(f32, rows, outs),
         vmem(f32, outs // LANES, rows, LANES),
         dma((9,)),
@@ -494,7 +500,7 @@
         dma((GROUPS, 2)),
         dma((GROUPS, 2)),
     ]
-    hbm = pl.BlockSpec(memory_space=pl.ANY)
+    hbm = pl.BlockSpec(memory_space=pltpu.HBM)
     return pl.pallas_call(
         functools.partial(kernel, nz),
         out_shape=jax.ShapeDtypeStruct((rows, outs), bf16),
@@ -502,18 +508,23 @@
         out_specs=pl.BlockSpec(memory_space=pltpu.VMEM),
         scratch_shapes=scratch,
         compiler_params=pltpu.CompilerParams(
-            collective_id=0, has_side_effects=True, vmem_limit_bytes=40 * 1024 * 1024
+            collective_id=0, has_side_effects=True, vmem_limit_bytes=48 * 1024 * 1024
         ),
     )(
-        gate_signal,
-        key_signal,
-        value_signal,
-        pole_decay,
-        pole_angle,
-        residue_real,
-        residue_imag,
-        skip_gain.reshape(1, width),
-        weight,
+        *(
+            pltpu.with_memory_space_constraint(array, pltpu.HBM)
+            for array in (
+                gate_signal,
+                key_signal,
+                value_signal,
+                pole_decay,
+                pole_angle,
+                residue_real,
+                residue_imag,
+                skip_gain.reshape(1, width),
+                weight,
+            )
+        )
     )
 
 

time: 45.4 us -> 34.7 us (0.76)
  the two profiles are of different devices: /device:TPU:33 before, /device:TPU:32 now
where the time goes in v2:
time: 34.7 us; the launch traced here: 34.6 us
  Pallas kernels  33.9 us (98%)
  local copies, waits for them, and re-layouts  0.71 us (2%)
    pallas_call x1, Pallas kernels, per_device(): pl.pallas_call(functools.partial(kernel, nz), out_shape=jax.ShapeDtypeStr...  33.9 us
    unnamed x1, local copies, waits for them, and re-layouts  0.71 us

profile of v2, /device:TPU:32, one launch (start us, length us, event | category | flops | bytes accessed | tf_op | source)
XLA Modules:
  0.0 34.6 jit_solution(15675154840283208688)
XLA Ops:
  0.0 33.9 %shard_map.91 = bf16[256,512]{1,0:T(8,128)(2,1)S(1)} custom-call(bf16[256,512]{1,0:T(8,128)(2,1)} %gate.1, bf16[256,512]{1,0:T(8,128)(2,1)} %key.1, bf16[256,512]{1,0:T(8,128)(2,1)} %value.1, f32[16,512]{1,0:T(8,128)} %decay.1, f32[16,512]{1,0:T(8,128)} %angle.1, f32[16,512]{1,0:T(8,128)} %res_real.1, f32[16,512]{1,0:T(8,128)} %res_imag.1, ...), custom_call_target="tpu_custom_call" | custom-call | tf_op jit(solution)/shard_map/pallas_call | solution.py:504
  33.9 0.7 %copy.11 = bf16[256,512]{1,0:T(8,128)(2,1)} copy(bf16[256,512]{1,0:T(8,128)(2,1)S(1)} %shard_map.91) | data formatting | bytes 524288

commit v3 on v2

--- a/solution.py
+++ b/solution.py
@@ -14,7 +14,7 @@
 BLOCKS = 8
 NX = 4
 NY = 4
-GROUP_ROWS = (64, 192)
+GROUP_ROWS = (64, 64, 128)
 GROUPS = len(GROUP_ROWS)
 
 
@@ -48,6 +48,7 @@
     imag_v,
     skip_v,
     w_all,
+    w_t,
     u,
     g_perm,
     power,
@@ -93,6 +94,7 @@
     up_recv,
     down_send,
     down_recv,
+    ready,
 ):
     rows, width = key_v.shape
     step = rows // BLOCKS
@@ -128,9 +130,25 @@
     barrier = pltpu.get_barrier_semaphore()
     peers = [sibling, up_dev, down_dev]
     peers += [{"ctx": z * NX + lax.rem(x + d, NX), "ch": ch} for d in range(1, NX)]
-    peers += [{"ctx": lax.rem(z + d, nz) * NX + x, "ch": ch} for d in range(1, nz)]
     for peer in peers:
         pl.semaphore_signal(barrier, inc=1, device_id=peer, device_id_type=MESH)
+    for d in range(1, nz):
+
+        @pl.when(z + d < nz)
+        def _():
+            later = {"ctx": (z + d) * NX + x, "ch": ch}
+            pl.semaphore_signal(barrier, inc=1, device_id=later, device_id_type=MESH)
+
+    pl.semaphore_wait(barrier, len(peers) + z)
+    for d in range(1, nz):
+
+        @pl.when(z >= d)
+        def _():
+            earlier = {"ctx": (z - d) * NX + x, "ch": ch}
+            pl.semaphore_signal(ready.at[d], inc=1, device_id=earlier, device_id_type=MESH)
+
+    w_copy = remote(weight.at[:, 1 - core], w_all.at[:, :, width:], wsib_sem.at[0], wsib_sem.at[1], sibling)
+    w_copy.start()
 
     loads[0].wait()
     loads[1].wait()
@@ -174,7 +192,6 @@
             drive = key_v[part, lanes(q)].astype(jnp.float32) * value_v[part, lanes(q)].astype(jnp.float32)
             u[q, pl.ds(8 * BLOCKS + b, step, stride=BLOCKS), :] = drive
 
-    w_copy = remote(weight.at[:, 1 - core], w_all.at[:, :, width:], wsib_sem.at[0], wsib_sem.at[1], sibling)
 
     def total_of(i, _):
         q = lax.rem(x + jnp.where(i == 0, 2, jnp.where(i == 1, 1, jnp.where(i == 2, 3, 0))), NX)
@@ -184,7 +201,7 @@
             return tuple(acc[k] + power[q, step - 1 - j, pl.ds(k, 1), :] * row for k in range(STATE))
 
         acc = lax.fori_loop(
-            0, step, add_token, tuple(jnp.zeros((BLOCKS, LANES), jnp.float32) for _ in range(STATE)), unroll=2
+            0, step, add_token, tuple(jnp.zeros((BLOCKS, LANES), jnp.float32) for _ in range(STATE)), unroll=8
         )
         for k in range(STATE):
             sums[q, pl.ds(k, BLOCKS, stride=STATE), :] = acc[k]
@@ -194,10 +211,6 @@
             state = advanced(lam, state) + sums[q, b * STATE : (b + 1) * STATE, :]
         tot[q] = state
 
-        @pl.when(i == 0)
-        def _():
-            pl.semaphore_wait(barrier, len(peers))
-
         @pl.when(i < NX - 1)
         def _():
             remote(
@@ -211,7 +224,6 @@
         return 0
 
     lax.fori_loop(0, quarters, total_of, 0)
-    w_copy.start()
 
     for i in (4, 5, 6):
         loads[i].wait()
@@ -243,11 +255,15 @@
             row_tot, row_in.at[z], row_send.at[d], row_recv.at[z], {"ctx": lax.rem(z + d, nz) * NX + x, "ch": ch}
         )
 
-    for d in reversed(range(1, nz)):
-
+    def send_row(d):
         @pl.when(z + d < nz)
         def _():
+            pl.semaphore_wait(ready.at[d], 1)
             row_copy(d).start()
+
+    by_distance = sorted(range(1, nz), key=lambda d: (min(d, nz - d), d))
+    for d in by_distance[:-1]:
+        send_row(d)
 
     loads[7].wait()
     chunk = 8 * BLOCKS
@@ -267,6 +283,8 @@
         for b in range(BLOCKS):
             part = slice(b * step, (b + 1) * step)
             g_perm[q, pl.ds(b, step, stride=BLOCKS), :] = gate_v[part, lanes(q)].astype(jnp.float32)
+
+    send_row(by_distance[-1])
 
     lam = lam_row[x]
     before[...] = jnp.zeros_like(before)
@@ -289,6 +307,14 @@
             start_out.at[to], start_in.at[x], start_send.at[d], start_recv.at[x], {"ctx": z * NX + to, "ch": ch}
         ).start()
     start_in[x] = start_out[x]
+
+    loads[8].wait()
+    for to in range(NY):
+        w_t[to, :width, :] = w_all[to, :, :width].T
+    w_copy.wait_recv()
+    for to in range(NY):
+        w_t[to, width:, :] = w_all[to, :, width:].T
+
     for d in range(1, NX):
         src = lax.rem(x + d, NX)
         remote(start_out.at[src], start_in.at[src], start_send.at[0], start_recv.at[src], sibling).wait_recv()
@@ -331,7 +357,7 @@
                 g_all[to, lanes(q)] = jnp.concatenate(done, axis=0).astype(jnp.bfloat16)
                 return 0
 
-            lax.fori_loop(at_rows.start // (2 * BLOCKS), at_rows.stop // (2 * BLOCKS), two_tokens, 0)
+            lax.fori_loop(at_rows.start // (2 * BLOCKS), at_rows.stop // (2 * BLOCKS), two_tokens, 0, unroll=4)
 
     def sib_copy(g):
         at = rows_of(g)
@@ -339,7 +365,7 @@
 
     def product(g, to):
         return lax.dot_general(
-            g_all[rows_of(g), :], w_all[to], (((1,), (1,)), ((), ())), preferred_element_type=jnp.float32
+            g_all[rows_of(g), :], w_t[to], (((1,), (0,)), ((), ())), preferred_element_type=jnp.float32
         )
 
     def far_copies(g):
@@ -381,21 +407,26 @@
         arrived[1].wait_recv()
         down_out[high, :] = (down_part[high, :] + far_in[high, :].astype(jnp.float32)).astype(jnp.bfloat16)
         down_copy(g, 1).start()
+
+    def keep_own(g):
         own_part[rows_of(g), :] = product(g, y)
 
-    for g in range(GROUPS + 1):
-        if g < GROUPS:
-            gated(g)
-            sib_copy(g).start()
-        if g == 0:
-            loads[8].wait()
-            w_copy.wait_recv()
-        if g > 0:
-            sib_copy(g - 1).wait_recv()
-            send_off(g - 1)
-        if g > 1:
-            send_rest(g - 2)
-    send_rest(GROUPS - 1)
+    for g in range(2):
+        gated(g)
+        sib_copy(g).start()
+    for g in range(2):
+        sib_copy(g).wait_recv()
+        send_off(g)
+    gated(2)
+    sib_copy(2).start()
+    send_rest(0)
+    keep_own(0)
+    sib_copy(2).wait_recv()
+    send_off(2)
+    send_rest(1)
+    send_rest(2)
+    keep_own(1)
+    keep_own(2)
 
     for g in range(GROUPS):
         for i in (1, 0):
@@ -454,6 +485,7 @@
         vmem(f32, MODES, width),
         vmem(f32, 1, width),
         vmem(bf16, NY, outs, 2 * width),
+        vmem(bf16, NY, 2 * width, outs),
         vmem(f32, quarters, 8 * BLOCKS + rows, LANES),
         vmem(f32, quarters, rows, LANES),
         vmem(f32, quarters, step + 1, STATE, LANES),
@@ -499,6 +531,7 @@
         dma((GROUPS, 2)),
         dma((GROUPS, 2)),
         dma((GROUPS, 2)),
+        pltpu.SemaphoreType.REGULAR((nz,)),
     ]
     hbm = pl.BlockSpec(memory_space=pltpu.HBM)
     return pl.pallas_call(

time: 34.7 us -> 32.2 us (0.928)
  the two profiles are of different devices: /device:TPU:32 before, /device:TPU:224 now
where the time goes in v3:
time: 32.2 us
  Pallas kernels  31.4 us (98%)
  local copies, waits for them, and re-layouts  0.71 us (2%)
    pallas_call x1, Pallas kernels, per_device(): pl.pallas_call(functools.partial(kernel, nz), out_shape=jax.ShapeDtypeStr...  31.4 us
    unnamed x1, local copies, waits for them, and re-layouts  0.71 us

profile of v3, /device:TPU:224, one launch (start us, length us, event | category | flops | bytes accessed | tf_op | source)
XLA Modules:
  0.0 32.2 jit_solution(13075965829097163135)
XLA Ops:
  0.0 31.4 %shard_map.91 = bf16[256,512]{1,0:T(8,128)(2,1)S(1)} custom-call(bf16[256,512]{1,0:T(8,128)(2,1)} %gate.1, bf16[256,512]{1,0:T(8,128)(2,1)} %key.1, bf16[256,512]{1,0:T(8,128)(2,1)} %value.1, f32[16,512]{1,0:T(8,128)} %decay.1, f32[16,512]{1,0:T(8,128)} %angle.1, f32[16,512]{1,0:T(8,128)} %res_real.1, f32[16,512]{1,0:T(8,128)} %res_imag.1, ...), custom_call_target="tpu_custom_call" | custom-call | tf_op jit(solution)/shard_map/pallas_call | solution.py:537
  31.4 0.7 %copy.11 = bf16[256,512]{1,0:T(8,128)(2,1)} copy(bf16[256,512]{1,0:T(8,128)(2,1)S(1)} %shard_map.91) | data formatting | bytes 524288

commit v4 on v3

--- a/solution.py
+++ b/solution.py
@@ -15,6 +15,7 @@
 NX = 4
 NY = 4
 GROUP_ROWS = (64, 64, 128)
+EARLY = 1
 GROUPS = len(GROUP_ROWS)
 
 
@@ -166,7 +167,7 @@
             power[q, j, MODES:, :] = pi[:, lanes(q)]
         return cmul(pr, pi, lam_r, lam_i)
 
-    pr, pi = lax.fori_loop(0, step, store_power, (jnp.ones_like(lam_r), jnp.zeros_like(lam_r)))
+    pr, pi = lax.fori_loop(0, step, store_power, (jnp.ones_like(lam_r), jnp.zeros_like(lam_r)), unroll=4)
     for q in range(quarters):
         power[q, step, :MODES, :] = pr[:, lanes(q)]
         power[q, step, MODES:, :] = pi[:, lanes(q)]
@@ -248,7 +249,7 @@
     state = tot_in[0]
     for i in range(1, NX):
         state = advanced(lam, state) + tot_in[i]
-    row_tot[...] = state
+    row_tot[...] = state.astype(row_tot.dtype)
 
     def row_copy(d):
         return remote(
@@ -261,7 +262,7 @@
             pl.semaphore_wait(ready.at[d], 1)
             row_copy(d).start()
 
-    by_distance = sorted(range(1, nz), key=lambda d: (min(d, nz - d), d))
+    by_distance = sorted(range(1, nz), key=lambda d: (2 * d == nz, -min(d, nz - d), d))
     for d in by_distance[:-1]:
         send_row(d)
 
@@ -293,7 +294,7 @@
         @pl.when(s < z)
         def _():
             remote(row_tot, row_in.at[s], row_send.at[0], row_recv.at[s], sibling).wait_recv()
-            before[...] = advanced(lam, before[...]) + row_in[s]
+            before[...] = advanced(lam, before[...]) + row_in[s].astype(jnp.float32)
 
     lam = lam_span[x]
     state = before[...]
@@ -315,11 +316,16 @@
     for to in range(NY):
         w_t[to, width:, :] = w_all[to, :, width:].T
 
-    for d in range(1, NX):
-        src = lax.rem(x + d, NX)
-        remote(start_out.at[src], start_in.at[src], start_send.at[0], start_recv.at[src], sibling).wait_recv()
-
-    for q in range(quarters):
+    def rows_of(g):
+        begin = sum(GROUP_ROWS[:g])
+        return slice(begin, begin + GROUP_ROWS[g])
+
+    def halves_of(g):
+        at = rows_of(g)
+        middle = (at.start + at.stop) // 2
+        return slice(at.start, middle), slice(middle, at.stop)
+
+    def block_states(q):
         lam = lam_block[q]
         state = start_in[q]
         for b in range(BLOCKS):
@@ -327,22 +333,14 @@
             if b < BLOCKS - 1:
                 state = advanced(lam, state) + sums[q, b * STATE : (b + 1) * STATE, :]
 
-    def rows_of(g):
-        begin = sum(GROUP_ROWS[:g])
-        return slice(begin, begin + GROUP_ROWS[g])
-
-    def halves_of(g):
-        at = rows_of(g)
-        middle = (at.start + at.stop) // 2
-        return slice(at.start, middle), slice(middle, at.stop)
-
-    def gated(g):
+    def gated(g, some=tuple(range(quarters))):
         at_rows = rows_of(g)
 
-        for q in range(quarters):
+        for q in some:
+            to_lanes = pl.ds(pl.multiple_of(q * LANES, LANES), LANES)
             held = [states[q, k * BLOCKS : (k + 1) * BLOCKS, :] for k in range(STATE)]
 
-            def two_tokens(i, _, q=q, held=held):
+            def two_tokens(i, _, q=q, held=held, to_lanes=to_lanes):
                 done = []
                 for t in range(2):
                     j = 2 * i + t
@@ -354,7 +352,7 @@
                     total = (partial[0] + partial[1]) + (partial[2] + partial[3])
                     done.append(total * g_perm[q, at, :])
                 to = pl.ds(pl.multiple_of(i * 2 * BLOCKS, 2 * BLOCKS), 2 * BLOCKS)
-                g_all[to, lanes(q)] = jnp.concatenate(done, axis=0).astype(jnp.bfloat16)
+                g_all[to, to_lanes] = jnp.concatenate(done, axis=0).astype(jnp.bfloat16)
                 return 0
 
             lax.fori_loop(at_rows.start // (2 * BLOCKS), at_rows.stop // (2 * BLOCKS), two_tokens, 0, unroll=4)
@@ -411,23 +409,31 @@
     def keep_own(g):
         own_part[rows_of(g), :] = product(g, y)
 
-    for g in range(2):
-        gated(g)
+    for d in (0, 1, 3, 2):
+        q = lax.rem(x + d, NX)
+        if d:
+            remote(start_out.at[q], start_in.at[q], start_send.at[0], start_recv.at[q], sibling).wait_recv()
+        block_states(q)
+        for g in range(EARLY):
+            gated(g, (q,))
+    for g in range(EARLY):
         sib_copy(g).start()
+    gated(1)
+    sib_copy(1).start()
     for g in range(2):
         sib_copy(g).wait_recv()
         send_off(g)
     gated(2)
     sib_copy(2).start()
     send_rest(0)
-    keep_own(0)
     sib_copy(2).wait_recv()
     send_off(2)
     send_rest(1)
     send_rest(2)
-    keep_own(1)
-    keep_own(2)
-
+    for g in range(GROUPS):
+        keep_own(g)
+
+    done = 0
     for g in range(GROUPS):
         for i in (1, 0):
             down_copy(g, 1 - i).wait_recv()
@@ -436,9 +442,13 @@
         whole = own_part[at, :] + up_in[at, :].astype(jnp.float32) + down_in[at, :].astype(jnp.float32)
         for q in range(quarters):
             final[q, at, :] = whole[:, lanes(q)]
-    for q in range(quarters):
-        for b in range(BLOCKS):
-            out[b * step : (b + 1) * step, lanes(q)] = final[q, pl.ds(b, step, stride=BLOCKS), :].astype(jnp.bfloat16)
+        while at.stop - done >= 16 * BLOCKS:
+            first = done // BLOCKS
+            for q in range(quarters):
+                for b in range(BLOCKS):
+                    tokens = final[q, pl.ds(done + b, 16, stride=BLOCKS), :]
+                    out[b * step + first : b * step + first + 16, lanes(q)] = tokens.astype(jnp.bfloat16)
+            done += 16 * BLOCKS
 
     w_copy.wait_send()
     for d in range(1, NX):
@@ -497,8 +507,8 @@
         vmem(f32, quarters, STATE * BLOCKS, LANES),
         vmem(f32, quarters, STATE, LANES),
         vmem(f32, NX, STATE, LANES),
-        vmem(f32, STATE, LANES),
-        vmem(f32, nz, STATE, LANES),
+        vmem(bf16, STATE, LANES),
+        vmem(bf16, nz, STATE, LANES),
         vmem(f32, STATE, LANES),
         vmem(f32, NX, STATE, LANES),
         vmem(f32, NX, STATE, LANES),

time: 32.2 us -> 31.4 us (0.975)
  Pallas kernels: 31.4 us -> 30.6 us
    pallas_call x1, Pallas kernels: 31.4 us -> 30.6 us  [per_device(): pl.pallas_call(functools.partial(kernel, nz), out_shape=jax.ShapeDtypeStr...]
where the time goes in v4:
time: 31.4 us; the launch traced here: 31.3 us
  Pallas kernels  30.6 us (97%)
  local copies, waits for them, and re-layouts  0.71 us (2%)
    pallas_call x1, Pallas kernels, per_device(): pl.pallas_call(functools.partial(kernel, nz), out_shape=jax.ShapeDtypeStr...  30.6 us
    unnamed x1, local copies, waits for them, and re-layouts  0.71 us

profile of v4, /device:TPU:224, one launch (start us, length us, event | category | flops | bytes accessed | tf_op | source)
XLA Modules:
  0.0 31.3 jit_solution(6877433577029796472)
XLA Ops:
  0.0 30.6 %shard_map.91 = bf16[256,512]{1,0:T(8,128)(2,1)S(1)} custom-call(bf16[256,512]{1,0:T(8,128)(2,1)} %gate.1, bf16[256,512]{1,0:T(8,128)(2,1)} %key.1, bf16[256,512]{1,0:T(8,128)(2,1)} %value.1, f32[16,512]{1,0:T(8,128)} %decay.1, f32[16,512]{1,0:T(8,128)} %angle.1, f32[16,512]{1,0:T(8,128)} %res_real.1, f32[16,512]{1,0:T(8,128)} %res_imag.1, ...), custom_call_target="tpu_custom_call" | custom-call | tf_op jit(solution)/shard_map/pallas_call | solution.py:547
  30.6 0.7 %copy.11 = bf16[256,512]{1,0:T(8,128)(2,1)} copy(bf16[256,512]{1,0:T(8,128)(2,1)S(1)} %shard_map.91) | data formatting | bytes 524288

commit v5 on v4

--- a/solution.py
+++ b/solution.py
@@ -21,6 +21,18 @@
 
 def cmul(ar, ai, br, bi):
     return ar * br - ai * bi, ar * bi + ai * br
+
+
+def half_turn(angle):
+    half = 0.5 * angle
+    square = half * half
+    sine, cosine = 1.0, 1.0
+    for n in range(6, 0, -1):
+        sine = 1.0 - square * (1.0 / (2 * n * (2 * n + 1))) * sine
+    for n in range(7, 0, -1):
+        cosine = 1.0 - square * (1.0 / (2 * n * (2 * n - 1))) * cosine
+    sine = half * sine
+    return 2.0 * sine * cosine, (cosine - sine) * (cosine + sine)
 
 
 def advanced(step, state):
@@ -154,8 +166,9 @@
     loads[0].wait()
     loads[1].wait()
     magnitude = jnp.exp(-decay_v[...])
-    lam_r = magnitude * jnp.cos(angle_v[...])
-    lam_i = magnitude * jnp.sin(angle_v[...])
+    sine, cosine = half_turn(angle_v[...])
+    lam_r = magnitude * cosine
+    lam_i = magnitude * sine
 
     def lanes(q):
         return slice(q * LANES, (q + 1) * LANES)
@@ -202,7 +215,7 @@
             return tuple(acc[k] + power[q, step - 1 - j, pl.ds(k, 1), :] * row for k in range(STATE))
 
         acc = lax.fori_loop(
-            0, step, add_token, tuple(jnp.zeros((BLOCKS, LANES), jnp.float32) for _ in range(STATE)), unroll=8
+            0, step, add_token, tuple(jnp.zeros((BLOCKS, LANES), jnp.float32) for _ in range(STATE)), unroll=32
         )
         for k in range(STATE):
             sums[q, pl.ds(k, BLOCKS, stride=STATE), :] = acc[k]
@@ -279,12 +292,14 @@
             local[q, c * chunk : (c + 1) * chunk, :] = acc
         return 0
 
-    lax.fori_loop(0, quarters, fir, 0)
     for q in range(quarters):
         for b in range(BLOCKS):
             part = slice(b * step, (b + 1) * step)
             g_perm[q, pl.ds(b, step, stride=BLOCKS), :] = gate_v[part, lanes(q)].astype(jnp.float32)
 
+    loads[8].wait()
+    for to in range(NY):
+        w_t[to, :width, :] = w_all[to, :, :width].T
     send_row(by_distance[-1])
 
     lam = lam_row[x]
@@ -309,9 +324,8 @@
         ).start()
     start_in[x] = start_out[x]
 
-    loads[8].wait()
-    for to in range(NY):
-        w_t[to, :width, :] = w_all[to, :, :width].T
+    lax.fori_loop(0, quarters, fir, 0)
+
     w_copy.wait_recv()
     for to in range(NY):
         w_t[to, width:, :] = w_all[to, :, width:].T

time: 31.4 us -> 31 us (0.987)
  Pallas kernels: 30.6 us -> 30.2 us
    pallas_call x1, Pallas kernels: 30.6 us -> 30.2 us  [per_device(): pl.pallas_call(functools.partial(kernel, nz), out_shape=jax.ShapeDtypeStr...]
where the time goes in v5:
time: 31 us
  Pallas kernels  30.2 us (97%)
  local copies, waits for them, and re-layouts  0.71 us (2%)
    pallas_call x1, Pallas kernels, per_device(): pl.pallas_call(functools.partial(kernel, nz), out_shape=jax.ShapeDtypeStr...  30.2 us
    unnamed x1, local copies, waits for them, and re-layouts  0.71 us

profile of v5, /device:TPU:224, one launch (start us, length us, event | category | flops | bytes accessed | tf_op | source)
XLA Modules:
  0.0 31.0 jit_solution(11378771733997491801)
XLA Ops:
  0.0 30.2 %shard_map.91 = bf16[256,512]{1,0:T(8,128)(2,1)S(1)} custom-call(bf16[256,512]{1,0:T(8,128)(2,1)} %gate.1, bf16[256,512]{1,0:T(8,128)(2,1)} %key.1, bf16[256,512]{1,0:T(8,128)(2,1)} %value.1, f32[16,512]{1,0:T(8,128)} %decay.1, f32[16,512]{1,0:T(8,128)} %angle.1, f32[16,512]{1,0:T(8,128)} %res_real.1, f32[16,512]{1,0:T(8,128)} %res_imag.1, ...), custom_call_target="tpu_custom_call" | custom-call | tf_op jit(solution)/shard_map/pallas_call | solution.py:561
  30.2 0.7 %copy.11 = bf16[256,512]{1,0:T(8,128)(2,1)} copy(bf16[256,512]{1,0:T(8,128)(2,1)S(1)} %shard_map.91) | data formatting | bytes 524288
